TPU v7x, 32 devices: a whole 2x2x4 slice. The times are simulated.
32 devices in a mesh: seq: 8 (over z, x), tp: 4 (over y, core).
Axes of the slice: x: 2, y: 2, z: 4, core: 2. Of those that a mesh axis runs over, the one named last changes fastest.
Arguments:
- tokens: bfloat16 [8192, 2048], P('seq', 'tp'), may hold values from -6 to 6
- w_inner: bfloat16 [2048, 2, 4096], P('seq', None, 'tp'), may hold values from -0.125 to 0.125
- w_states: bfloat16 [2048, 256], P('seq'), may hold values from -0.125 to 0.125
- w_step: bfloat16 [2048, 64], P('seq', 'tp'), may hold values from -0.125 to 0.125
- conv_inner: float32 [4, 4096], P(None, 'tp'), may hold values from -3 to 3
- conv_states: float32 [4, 256], replicated, may hold values from -3 to 3
- decay_rate: float32 [64], P('tp'), may hold values from 0 to 1, as said below
- step_bias: float32 [64], P('tp'), may hold values from -1 to 0.5
- skip_gain: float32 [64], P('tp'), may hold values from 0.5 to 1.5
- norm_gain: float32 [4096], P('tp'), may hold values from 0.5 to 1.5
- w_output: bfloat16 [4096, 2048], P('tp', 'seq'), may hold values from -0.09375 to 0.09375
- block_owner: int32 [32], replicated, may hold values from 0 to 4, as said below
- lengths: int32 [5], replicated, may hold values from 1 to 4096, as said below
Outputs:
- mixed: bfloat16 [8192, 2048], P('seq', 'tp')
Inputs may be any that keep to these rules, and one draw needn't show every extreme that they name: `block_owner`: each prompt's blocks are consecutive, prompt r has ceil(lengths[r] / 256) of them, and the prompts follow one another in an order drawn afresh; one prompt has 16 blocks and is neither the first nor the last in that order. `lengths`: one prompt has exactly 4096 tokens. `decay_rate`: Positive.
All inputs are finite; a program needn't handle non-finite values.
Results may differ from a plain program's by a relative error of at most 0.0075.
Values may be sent and summed in bfloat16 or wider, within the bound.
A program may use at most 64 MiB of HBM per device.

v0:
```python
import jax
import jax.numpy as jnp
from jax import lax
from jax.sharding import PartitionSpec as P

BLOCK = 256


def passed_along(value, axis, by):
    count = lax.axis_size(axis)
    pairs = [(i, i + by) for i in range(count) if 0 <= i + by < count]
    return lax.ppermute(value, axis, pairs)


def convolve(values, edge_rows, weights, in_block, carry_on):
    lag_rows = weights.shape[0] - 1
    row_total = values.shape[0]
    widened = jnp.concatenate([edge_rows, values], axis=0).astype(jnp.float32)
    total = jnp.zeros(values.shape, jnp.float32)
    for offset in range(weights.shape[0]):
        shifted = widened[lag_rows - offset : lag_rows - offset + row_total]
        keeping = (in_block >= offset) | carry_on
        total = total + jnp.where(keeping[:, None], shifted, 0.0) * weights[offset]
    return jax.nn.silu(total).astype(jnp.bfloat16)


def on_device(
    tokens,
    w_inner,
    w_states,
    w_step,
    conv_inner,
    conv_states,
    decay_rate,
    step_bias,
    skip_gain,
    norm_gain,
    w_output,
    block_owner,
    lengths,
):
    row_count = tokens.shape[0]
    local_blocks = row_count // BLOCK
    total_blocks = block_owner.shape[0]
    heads_here = w_step.shape[1]
    inner_here = w_inner.shape[2]
    state_size = w_states.shape[1] // 2
    head_size = inner_here // heads_here
    lag_rows = conv_inner.shape[0] - 1
    block_ids = jnp.arange(total_blocks, dtype=jnp.int32)
    same_owner = block_owner[:, None] == block_owner[None, :]
    first_block = jnp.min(jnp.where(same_owner, block_ids[None, :], total_blocks), axis=1)
    starting = (first_block == block_ids).astype(jnp.int32)
    request_ids = jnp.arange(lengths.shape[0], dtype=jnp.int32)
    own_length = jnp.sum(
        jnp.where(block_owner[:, None] == request_ids[None, :], lengths[None, :], 0), axis=1
    )
    valid_rows = jnp.clip(own_length - (block_ids - first_block) * BLOCK, 0, BLOCK)
    seq_index = lax.axis_index("seq")
    local_start = lax.dynamic_slice_in_dim(starting, seq_index * local_blocks, local_blocks)
    local_valid = lax.dynamic_slice_in_dim(valid_rows, seq_index * local_blocks, local_blocks)
    in_block = jnp.arange(row_count, dtype=jnp.int32) % BLOCK
    carry_on = jnp.repeat(local_start == 0, BLOCK)
    whole = lax.all_gather(tokens, "tp", axis=1, tiled=True)
    pieces = (
        lax.all_gather(w_inner, "seq", axis=0, tiled=True),
        lax.all_gather(w_states, "seq", axis=0, tiled=True),
        lax.all_gather(w_step, "seq", axis=0, tiled=True),
    )
    count = pieces[0].shape[0]
    inner_sum = jnp.dot(
        whole, pieces[0].reshape(count, 2 * inner_here), preferred_element_type=jnp.float32
    )
    states_sum = jnp.dot(whole, pieces[1], preferred_element_type=jnp.float32)
    step_sum = jnp.dot(whole, pieces[2], preferred_element_type=jnp.float32)
    projected = inner_sum.astype(jnp.bfloat16)
    gate_in = projected[:, :inner_here]
    x_in = projected[:, inner_here:]
    bc_in = states_sum.astype(jnp.bfloat16)
    step_raw = step_sum.astype(jnp.bfloat16)
    edge_inner, edge_states = passed_along(
        (x_in[row_count - lag_rows :], bc_in[row_count - lag_rows :]), "seq", 1
    )
    x_conv = convolve(x_in, edge_inner, conv_inner, in_block, carry_on)
    bc_conv = convolve(bc_in, edge_states, conv_states, in_block, carry_on)
    step_size = jax.nn.softplus(step_raw.astype(jnp.float32) + step_bias)
    log_decay = -decay_rate * step_size
    x_heads = x_conv.reshape(local_blocks, BLOCK, heads_here, head_size)
    b_rows = bc_conv[:, :state_size].reshape(local_blocks, BLOCK, state_size)
    c_rows = bc_conv[:, state_size:].reshape(local_blocks, BLOCK, state_size)
    step_blocks = step_size.reshape(local_blocks, BLOCK, heads_here)
    cumulative = jnp.cumsum(log_decay.reshape(local_blocks, BLOCK, heads_here), axis=1)
    causal = jnp.arange(BLOCK)[:, None] >= jnp.arange(BLOCK)[None, :]
    spread = cumulative[:, :, None, :] - cumulative[:, None, :, :]
    decays = jnp.exp(jnp.where(causal[None, :, :, None], spread, -jnp.inf))
    intersection = jnp.einsum("cin,cjn->cij", c_rows, b_rows, preferred_element_type=jnp.float32)
    mixing = (decays * intersection[:, :, :, None] * step_blocks[:, None, :, :]).astype(
        jnp.bfloat16
    )
    y_inner = jnp.einsum("cijh,cjhp->cihp", mixing, x_heads, preferred_element_type=jnp.float32)
    final_log = cumulative[:, -1, :]
    tail_weight = jnp.exp(final_log[:, None, :] - cumulative) * step_blocks
    weighted_b = (tail_weight[:, :, :, None] * b_rows.astype(jnp.float32)[:, :, None, :]).astype(
        jnp.bfloat16
    )
    fresh = jnp.einsum("cjhn,cjhp->chnp", weighted_b, x_heads, preferred_element_type=jnp.float32)
    keep_flag = jnp.where(local_start == 1, 0.0, 1.0).astype(jnp.float32)
    block_gain_each = jnp.exp(final_log) * keep_flag[:, None]

    def fold_block(carry, item):
        gain_now, fresh_now = item
        return ((carry[0] * gain_now, gain_now[:, None, None] * carry[1] + fresh_now), None)

    zero_state = jnp.zeros((heads_here, state_size, head_size), jnp.float32)
    unit_gain = jnp.ones((heads_here,), jnp.float32)
    (block_gain, block_state), _ = lax.scan(
        fold_block, (unit_gain, zero_state), (block_gain_each, fresh)
    )

    def relay(iteration, entering_now):
        return passed_along(block_gain[:, None, None] * entering_now + block_state, "seq", 1)

    entering = lax.fori_loop(0, lax.axis_size("seq") - 1, relay, zero_state)

    def pass_block(previous, item):
        log_now, keep_now, fresh_now = item
        incoming = previous * keep_now
        return (jnp.exp(log_now)[:, None, None] * incoming + fresh_now, incoming)

    _, incoming_all = lax.scan(pass_block, entering, (final_log, keep_flag, fresh))
    incoming_half = incoming_all.astype(jnp.bfloat16)
    y_carry = jnp.exp(cumulative)[:, :, :, None] * jnp.einsum(
        "cin,chnp->cihp", c_rows, incoming_half, preferred_element_type=jnp.float32
    )
    y_total = (y_inner + y_carry).reshape(row_count, inner_here) + jnp.repeat(skip_gain, head_size)[
        None, :
    ] * x_conv.astype(jnp.float32)
    gated = y_total * jax.nn.silu(gate_in.astype(jnp.float32))
    squares = lax.psum(jnp.sum(gated * gated, axis=1), "tp")
    square_mean = squares / (inner_here * lax.axis_size("tp"))
    normed = (gated * lax.rsqrt(square_mean + 1e-05)[:, None] * norm_gain).astype(jnp.bfloat16)
    partial_out = jnp.dot(
        normed,
        lax.all_gather(w_output, "seq", axis=1, tiled=True),
        preferred_element_type=jnp.float32,
    )
    summed = lax.psum_scatter(partial_out, "tp", scatter_dimension=1, tiled=True)
    live = in_block < jnp.repeat(local_valid, BLOCK)
    return jnp.where(live[:, None], summed, 0.0).astype(jnp.bfloat16)


def solution(mesh):
    return jax.shard_map(
        on_device,
        mesh=mesh,
        in_specs=(
            P("seq", "tp"),
            P("seq", None, "tp"),
            P("seq", None),
            P("seq", "tp"),
            P(None, "tp"),
            P(),
            P("tp"),
            P("tp"),
            P("tp"),
            P("tp"),
            P("tp", "seq"),
            P(),
            P(),
        ),
        out_specs=P("seq", "tp"),
        check_vma=False,
    )
```

profile of v0, /device:TPU:26, one launch (start us, length us, event | category | flops | bytes accessed | tf_op | source)
XLA Modules:
  0.0 541.3 jit_solution(18261094685388416830)
XLA Ops:
  14.1 30.9 %all_gather.17 = bf16[2048,16]{0,1:T(8,128)(2,1)S(1)} all-gather(bf16[256,16]{0,1:T(8,128)(2,1)} %param.22), channel_id=1, replica_groups=mesh['seq'=8,'tp'=4] {'seq'}, dimensions={0}, use_global_device_ids=true | all-gather | bytes 73728 | tf_op jit(solution)/shard_map/all_gather | solution.py:68
  48.7 37.0 %all-gather.5.cloned.1.call-done = bf16[1024,2048]{1,0:T(8,128)(2,1)} async-done(((bf16[1024,512]{1,0:T(8,128)(2,1)}), bf16[1024,2048]{1,0:T(8,128)(2,1)}) %all-gather.5.cloned.1.call-update) | async-done | bytes 4194320 | tf_op jit(solution)/shard_map/all_gather | solution.py:64
  98.6 111.3 %all-gather.7.cloned.1.call-done = bf16[2048,2,1024]{2,1,0:T(2,128)(2,1)} async-done(((bf16[256,2,1024]{2,1,0:T(2,128)(2,1)}), bf16[2048,2,1024]{2,1,0:T(2,128)(2,1)}) %all-gather.7.cloned.1.call-update) | async-done | bytes 8388624 | tf_op jit(solution)/shard_map/all_gather | solution.py:66
  209.9 10.2 %copy.102 = bf16[256,8,2,1024]{3,1,2,0:T(8,128)(2,1)} copy(bf16[256,8,2,1024]{3,2,1,0:T(2,128)(2,1)} %bitcast.93) | data formatting | bytes 16777216
  220.0 12.9 %convolution_convert_fusion = bf16[1024,2048]{1,0:T(8,128)(2,1)S(1)} fusion(bf16[1024,2048]{1,0:T(8,128)(2,1)} %all-gather.5.cloned.1.call-done, bf16[2048,2048]{1,0:T(8,128)(2,1)} %bitcast.94), kind=kOutput, calls=%fused_computation.44 | convolution fusion | flops 8592031744 | bytes 16777216 | tf_op jit(solution)/shard_map/dot_general | solution.py:71
  249.1 4.9 copy.82
  254.0 7.5 %fusion.14 = f32[4,16,128,64]{3,2,1,0:T(8,128)} fusion(bf16[4,256,16,64]{1,3,2,0:T(8,128)(2,1)S(1)} %copy.82, f32[4,256,128]{2,1,0:T(8,128)} %convert_element_type.65, f32[4,256,16]{1,2,0:T(8,128)S(1)} %get-tuple-element.209), kind=kOutput, calls=%fused_computation.26 | convolution fusion | flops 272629760 | bytes 4784128 | tf_op jit(solution)/shard_map/cjhn,cjhp->chnp/dot_general | solution.py:106
  261.5 8.5 %while.37 = (s32[]{:T(128)}, f32[16]{0:T(128)S(1)}, f32[16,128,64]{2,1,0:T(8,128)S(1)}, f32[4,16]{1,0:T(4,128)}, f32[4,16,128,64]{3,2,1,0:T(8,128)}, /*index=5*/s32[]{:T(128)}, s32[]{:T(128)}) while((s32[]{:T(128)}, f32[16]{0:T(128)S(1)}, f32[16,128,64]{2,1,0:T(8,128)S(1)}, f32[4,16]{1,0:T(4,128)}, f32[4,16,128,64]{3,2,1,0:T(8,128)}, ...), condition=%wide.region_5.6_spmd.clone, body=%wide.region_4.5_spmd.clone.sunk | while | flops 393251 | bytes 1573280 | solution.py:116
  270.5 106.6 %while.35 = (s32[]{:T(128)}, f32[16,128,64]{1,2,0:T(8,128)S(1)}, f32[16]{0:T(128)S(1)}, f32[16,128,64]{1,2,0:T(8,128)S(1)}, s32[]{:T(128)}) while((s32[]{:T(128)}, f32[16,128,64]{1,2,0:T(8,128)S(1)}, f32[16]{0:T(128)S(1)}, f32[16,128,64]{1,2,0:T(8,128)S(1)}, s32[]{:T(128)}) %tuple.79), condition=%wide.region_7.8_spmd, body=%wide.region_6.7_spmd.sunk | while | flops 262146 | bytes 3670181 | solution.py:123
  271.9 14.0 %collective-permute-done = f32[16,128,64]{1,2,0:T(8,128)S(1)} collective-permute-done((f32[16,128,64]{1,2,0:T(8,128)S(1)}, f32[16,128,64]{1,2,0:T(8,128)S(1)}, u32[]{:S(2)}, u32[]{:S(2)}) %collective-permute-start) | collective-permute-done | bytes 524320 | tf_op jit(solution)/shard_map/while/body/eval_jaxpr/ppermute | solution.py:12
  287.4 23.4 %collective-permute-done = f32[16,128,64]{1,2,0:T(8,128)S(1)} collective-permute-done((f32[16,128,64]{1,2,0:T(8,128)S(1)}, f32[16,128,64]{1,2,0:T(8,128)S(1)}, u32[]{:S(2)}, u32[]{:S(2)}) %collective-permute-start) | collective-permute-done | bytes 524320 | tf_op jit(solution)/shard_map/while/body/eval_jaxpr/ppermute | solution.py:12
  312.2 13.5 %collective-permute-done = f32[16,128,64]{1,2,0:T(8,128)S(1)} collective-permute-done((f32[16,128,64]{1,2,0:T(8,128)S(1)}, f32[16,128,64]{1,2,0:T(8,128)S(1)}, u32[]{:S(2)}, u32[]{:S(2)}) %collective-permute-start) | collective-permute-done | bytes 524320 | tf_op jit(solution)/shard_map/while/body/eval_jaxpr/ppermute | solution.py:12
  327.1 12.6 %collective-permute-done = f32[16,128,64]{1,2,0:T(8,128)S(1)} collective-permute-done((f32[16,128,64]{1,2,0:T(8,128)S(1)}, f32[16,128,64]{1,2,0:T(8,128)S(1)}, u32[]{:S(2)}, u32[]{:S(2)}) %collective-permute-start) | collective-permute-done | bytes 524320 | tf_op jit(solution)/shard_map/while/body/eval_jaxpr/ppermute | solution.py:12
  341.1 11.7 %collective-permute-done = f32[16,128,64]{1,2,0:T(8,128)S(1)} collective-permute-done((f32[16,128,64]{1,2,0:T(8,128)S(1)}, f32[16,128,64]{1,2,0:T(8,128)S(1)}, u32[]{:S(2)}, u32[]{:S(2)}) %collective-permute-start) | collective-permute-done | bytes 524320 | tf_op jit(solution)/shard_map/while/body/eval_jaxpr/ppermute | solution.py:12
  354.3 10.8 %collective-permute-done = f32[16,128,64]{1,2,0:T(8,128)S(1)} collective-permute-done((f32[16,128,64]{1,2,0:T(8,128)S(1)}, f32[16,128,64]{1,2,0:T(8,128)S(1)}, u32[]{:S(2)}, u32[]{:S(2)}) %collective-permute-start) | collective-permute-done | bytes 524320 | tf_op jit(solution)/shard_map/while/body/eval_jaxpr/ppermute | solution.py:12
  366.4 10.7 %collective-permute-done = f32[16,128,64]{1,2,0:T(8,128)S(1)} collective-permute-done((f32[16,128,64]{1,2,0:T(8,128)S(1)}, f32[16,128,64]{1,2,0:T(8,128)S(1)}, u32[]{:S(2)}, u32[]{:S(2)}) %collective-permute-start) | collective-permute-done | bytes 524320 | tf_op jit(solution)/shard_map/while/body/eval_jaxpr/ppermute | solution.py:12
  377.5 20.2 %while.36 = (s32[]{:T(128)}, f32[16,128,64]{2,1,0:T(8,128)S(1)}, bf16[4,16,128,64]{3,2,1,0:T(8,128)(2,1)}, f32[4,16]{1,0:T(4,128)}, f32[4]{0:T(128)S(1)}, /*index=5*/f32[4,16,128,64]{3,2,1,0:T(8,128)}, s32[]{:T(128)}) while((s32[]{:T(128)}, f32[16,128,64]{2,1,0:T(8,128)S(1)}, bf16[4,16,128,64]{3,2,1,0:T(8,128)(2,1)}, f32[4,16]{1,0:T(4,128)}, ...), condition=%wide.region_9.10_spmd, body=%wide.region_8.9_spmd.sunk | while | flops 524290 | bytes 3147045 | solution.py:130
  401.1 6.2 %bitcast_add_fusion.2 = f32[4,256,16,64]{1,3,2,0:T(8,128)} fusion(f32[4,256,16,64]{1,3,2,0:T(8,128)S(1)} %bitcast.95, bf16[4,256,16,64]{1,3,2,0:T(8,128)(2,1)S(1)} %copy-done.2, f32[4,256,16]{1,2,0:T(8,128)S(1)} %bitcast.104, f32[4,256,256]{2,1,0:T(8,128)S(1)} %copy-done.5, f32[4,256,16]{1,2,0:T(8,128)S(1)} %bitcast_bitcast_fusion, ...), kind=kOutput, calls=%fused_computation.38 | convolution fusion | flops 559939584 | bytes 11796480 | tf_op jit(solution)/shard_map/cijh,cjhp->cihp/dot_general | solution.py:100
  407.3 8.1 %copy.93 = f32[4,256,16,64]{3,2,1,0:T(8,128)} copy(f32[4,256,16,64]{1,3,2,0:T(8,128)} %bitcast_add_fusion.2) | data formatting | bytes 8388608 | tf_op jit(solution)/shard_map/reshape | solution.py:135
  415.5 7.6 %reshape.135 = f32[1024,1024]{1,0:T(8,128)} reshape(f32[4,256,16,64]{3,2,1,0:T(8,128)} %copy.93) | data formatting | bytes 8388608 | tf_op jit(solution)/shard_map/reshape | solution.py:135
  423.1 15.2 %multiply_reduce_fusion = (f32[1024]{0:T(1024)S(1)}, f32[1024,1024]{1,0:T(8,128)}) fusion(bf16[1024,2048]{1,0:T(8,128)(2,1)} %copy-done.4, f32[1024,1024]{1,0:T(8,128)} %reshape.135, f32[1024]{0:T(1024)S(1)} %copy-done.24, f32[1024]{0:T(1024)S(1)} %bitcast.110, f32[1027,1024]{1,0:T(8,128)} %copy-done, pred[1024]{0:T(1024)(128)(4,1)S(1)} %copy-done.17, ...), kind=kLoop, calls=%fused_computation.40 | loop fusion | flops 28310528 | bytes 27291648 | tf_op jit(solution)/shard_map/reduce_sum | solution.py:139
  438.4 6.1 %psum.7 = f32[1024]{0:T(1024)S(1)} all-reduce(f32[1024]{0:T(1024)S(1)} %get-tuple-element.204), channel_id=1, replica_groups=mesh['seq'=8,'tp'=4] {'tp'}, use_global_device_ids=true, to_apply=%region_11.12 | all-reduce | flops 1024 | bytes 8192 | tf_op jit(solution)/shard_map/psum | solution.py:139
  444.5 11.3 %fusion.24 = f32[1024,2048]{1,0:T(8,128)} fusion(bf16[1024,2048]{1,0:T(8,128)(2,1)} %all-gather.11.cloned.1.call-done, f32[1024,1024]{1,0:T(8,128)} %get-tuple-element.205, f32[1024]{0:T(1024)S(1)} %copy-done.28, f32[1024]{0:T(1024)S(1)} %add_rsqrt_fusion), kind=kOutput, calls=%fused_computation.46 | convolution fusion | flops 4298113024 | bytes 16785408 | tf_op jit(solution)/shard_map/dot_general | solution.py:142
  456.7 75.3 %reduce-scatter.2.cloned.1.call-done = f32[1024,512]{1,0:T(8,128)} async-done(((f32[1024,2048]{1,0:T(8,128)}), f32[1024,512]{1,0:T(8,128)}) %reduce-scatter.2.cloned.1.call-update) | async-done | bytes 2097168 | tf_op jit(solution)/shard_map/reduce_scatter | solution.py:147
  (174 shorter events, 86.2 us)
Async XLA Ops:
  6.5 42.2 %all-gather.9.cloned.1.call-start = ((), (), s32[]{:S(2)}) async-start(), calls=%async_computation.3 | async-start | bytes 1179648 | tf_op jit(solution)/shard_map/all_gather | solution.py:67
  7.3 78.4 %all-gather.5.cloned.1.call-start = ((), (), s32[]{:S(2)}) async-start(), calls=%async_computation.1 | async-start | bytes 5242880 | tf_op jit(solution)/shard_map/all_gather | solution.py:64
  8.0 201.9 %all-gather.7.cloned.1.call-start = ((), (), s32[]{:S(2)}) async-start(), calls=%async_computation.2 | async-start | bytes 9437184 | tf_op jit(solution)/shard_map/all_gather | solution.py:66
  8.7 82.2 %copy-start.25 = (f32[16]{0:T(128)S(1)}, f32[16]{0:T(128)}, u32[]{:S(2)}) copy-start(f32[16]{0:T(128)} %param.26) | copy-start | bytes 196
  8.8 435.7 %all-gather.11.cloned.1.call-start = ((), (), s32[]{:S(2)}) async-start(), calls=%async_computation.4 | async-start | bytes 4718592 | tf_op jit(solution)/shard_map/all_gather | solution.py:144
  9.3 522.7 %reduce-scatter.2.cloned.1.call-start = ((), (), s32[]{:S(2)}) async-start(), calls=%async_computation.5 | async-start | bytes 10485760 | tf_op jit(solution)/shard_map/reduce_scatter | solution.py:147
  11.0 84.7 %copy-start.26 = (f32[4]{0:T(128)}, f32[4]{0:T(128)S(1)}, u32[]{:S(2)}) copy-start(f32[4]{0:T(128)S(1)} %compare_select_fusion.1) | copy-start | bytes 52
  11.7 85.3 %copy-start.12 = (pred[1024]{0:T(1024)(128)(4,1)}, pred[1024]{0:T(1024)(128)(4,1)S(1)}, u32[]{:S(2)}) copy-start(pred[1024]{0:T(1024)(128)(4,1)S(1)} %get-tuple-element.218) | copy-start | bytes 3076
  11.7 85.4 %copy-start.15 = (pred[1024]{0:T(1024)(128)(4,1)}, pred[1024]{0:T(1024)(128)(4,1)S(1)}, u32[]{:S(2)}) copy-start(pred[1024]{0:T(1024)(128)(4,1)S(1)} %get-tuple-element.219) | copy-start | bytes 3076
  11.7 85.4 %copy-start.18 = (pred[1024]{0:T(1024)(128)(4,1)}, pred[1024]{0:T(1024)(128)(4,1)S(1)}, u32[]{:S(2)}) copy-start(pred[1024]{0:T(1024)(128)(4,1)S(1)} %get-tuple-element.220) | copy-start | bytes 3076
  11.8 85.4 %copy-start.21 = (pred[1024]{0:T(1024)(128)(4,1)}, pred[1024]{0:T(1024)(128)(4,1)S(1)}, u32[]{:S(2)}) copy-start(pred[1024]{0:T(1024)(128)(4,1)S(1)} %get-tuple-element.221) | copy-start | bytes 3076
  89.6 7.3 %collective-permute-start.2 = (bf16[3,256]{1,0:T(4,128)(2,1)S(1)}, bf16[3,256]{1,0:T(4,128)(2,1)S(1)}, u32[]{:S(2)}, u32[]{:S(2)}) collective-permute-start(bf16[3,256]{1,0:T(4,128)(2,1)S(1)} %slice.109), channel_id=1, source_target_pairs={{0,4},{4,8},{8,12},{12,16},{16,20},{20,24},{24,28},{1,5},{5,9},{9,... | collective-permute-start | bytes 4616 | tf_op jit(solution)/shard_map/ppermute | solution.py:12
  232.9 5.5 %collective-permute-start.1 = (bf16[3,1024]{1,0:T(4,128)(2,1)S(1)}, bf16[3,1024]{1,0:T(4,128)(2,1)S(1)}, u32[]{:S(2)}, u32[]{:S(2)}) collective-permute-start(bf16[3,1024]{1,0:T(4,128)(2,1)S(1)} %slice.101), channel_id=1, source_target_pairs={{0,4},{4,8},{8,12},{12,16},{16,20},{20,24},{24,28},{1,5},{5,9},{9,... | collective-permute-start | bytes 18440 | tf_op jit(solution)/shard_map/ppermute | solution.py:12
  270.5 107.0 %copy-start.27 = (f32[4]{0:T(128)S(1)}, f32[4]{0:T(128)}, u32[]{:S(2)}) copy-start(f32[4]{0:T(128)} %copy-done.26) | copy-start | bytes 52
  270.6 15.3 %collective-permute-start = (f32[16,128,64]{1,2,0:T(8,128)S(1)}, f32[16,128,64]{1,2,0:T(8,128)S(1)}, u32[]{:S(2)}, u32[]{:S(2)}) collective-permute-start(f32[16,128,64]{1,2,0:T(8,128)S(1)} %multiply_add_fusion.2), channel_id=1, source_target_pairs={{0,4},{4,8},{8,12},{12,16},{16,20},{20,24},{24,28},{1,5},{5,9},{9,... | collective-permute-start | bytes 1572872 | tf_op jit(solution)/shard_map/while/body/eval_jaxpr/ppermute | solution.py:12
  286.0 24.7 %collective-permute-start = (f32[16,128,64]{1,2,0:T(8,128)S(1)}, f32[16,128,64]{1,2,0:T(8,128)S(1)}, u32[]{:S(2)}, u32[]{:S(2)}) collective-permute-start(f32[16,128,64]{1,2,0:T(8,128)S(1)} %multiply_add_fusion.2), channel_id=1, source_target_pairs={{0,4},{4,8},{8,12},{12,16},{16,20},{20,24},{24,28},{1,5},{5,9},{9,... | collective-permute-start | bytes 1572872 | tf_op jit(solution)/shard_map/while/body/eval_jaxpr/ppermute | solution.py:12
  310.9 14.8 %collective-permute-start = (f32[16,128,64]{1,2,0:T(8,128)S(1)}, f32[16,128,64]{1,2,0:T(8,128)S(1)}, u32[]{:S(2)}, u32[]{:S(2)}) collective-permute-start(f32[16,128,64]{1,2,0:T(8,128)S(1)} %multiply_add_fusion.2), channel_id=1, source_target_pairs={{0,4},{4,8},{8,12},{12,16},{16,20},{20,24},{24,28},{1,5},{5,9},{9,... | collective-permute-start | bytes 1572872 | tf_op jit(solution)/shard_map/while/body/eval_jaxpr/ppermute | solution.py:12
  325.8 13.9 %collective-permute-start = (f32[16,128,64]{1,2,0:T(8,128)S(1)}, f32[16,128,64]{1,2,0:T(8,128)S(1)}, u32[]{:S(2)}, u32[]{:S(2)}) collective-permute-start(f32[16,128,64]{1,2,0:T(8,128)S(1)} %multiply_add_fusion.2), channel_id=1, source_target_pairs={{0,4},{4,8},{8,12},{12,16},{16,20},{20,24},{24,28},{1,5},{5,9},{9,... | collective-permute-start | bytes 1572872 | tf_op jit(solution)/shard_map/while/body/eval_jaxpr/ppermute | solution.py:12
  339.8 13.0 %collective-permute-start = (f32[16,128,64]{1,2,0:T(8,128)S(1)}, f32[16,128,64]{1,2,0:T(8,128)S(1)}, u32[]{:S(2)}, u32[]{:S(2)}) collective-permute-start(f32[16,128,64]{1,2,0:T(8,128)S(1)} %multiply_add_fusion.2), channel_id=1, source_target_pairs={{0,4},{4,8},{8,12},{12,16},{16,20},{20,24},{24,28},{1,5},{5,9},{9,... | collective-permute-start | bytes 1572872 | tf_op jit(solution)/shard_map/while/body/eval_jaxpr/ppermute | solution.py:12
  353.0 12.1 %collective-permute-start = (f32[16,128,64]{1,2,0:T(8,128)S(1)}, f32[16,128,64]{1,2,0:T(8,128)S(1)}, u32[]{:S(2)}, u32[]{:S(2)}) collective-permute-start(f32[16,128,64]{1,2,0:T(8,128)S(1)} %multiply_add_fusion.2), channel_id=1, source_target_pairs={{0,4},{4,8},{8,12},{12,16},{16,20},{20,24},{24,28},{1,5},{5,9},{9,... | collective-permute-start | bytes 1572872 | tf_op jit(solution)/shard_map/while/body/eval_jaxpr/ppermute | solution.py:12
  365.1 12.0 %collective-permute-start = (f32[16,128,64]{1,2,0:T(8,128)S(1)}, f32[16,128,64]{1,2,0:T(8,128)S(1)}, u32[]{:S(2)}, u32[]{:S(2)}) collective-permute-start(f32[16,128,64]{1,2,0:T(8,128)S(1)} %multiply_add_fusion.2), channel_id=1, source_target_pairs={{0,4},{4,8},{8,12},{12,16},{16,20},{20,24},{24,28},{1,5},{5,9},{9,... | collective-permute-start | bytes 1572872 | tf_op jit(solution)/shard_map/while/body/eval_jaxpr/ppermute | solution.py:12
  415.4 7.7 %copy-start.23 = (pred[1024]{0:T(1024)(128)(4,1)S(1)}, pred[1024]{0:T(1024)(128)(4,1)}, u32[]{:S(2)}) copy-start(pred[1024]{0:T(1024)(128)(4,1)} %copy-done.21) | copy-start | bytes 3076
  415.4 7.7 %copy-start.24 = (f32[1024]{0:T(1024)S(1)}, f32[1024]{0:T(1024)}, u32[]{:S(2)}) copy-start(f32[1024]{0:T(1024)} %mul.265) | copy-start | bytes 12292
  423.1 21.4 %copy-start.28 = (f32[1024]{0:T(1024)S(1)}, f32[1024]{0:T(1024)}, u32[]{:S(2)}) copy-start(f32[1024]{0:T(1024)} %param.28) | copy-start | bytes 12292
  (23 other events, 87.9 us)
Sparse Core Ops, SparseCore 0:
  9.5 39.1 all-gather.8
  50.3 35.3 all-gather.4
  87.8 121.9 all-gather.6
  211.8 78.1 all-gather.10
  455.9 76.0 reduce-scatter.1
where the time goes:
time: 545 us; the launch traced here: 541 us
  waiting for transfers between devices  326 us (60%)
  other arithmetic  55.4 us (10%)
  local copies, waits for them, and re-layouts  51.8 us (10%)
  matrix products  45 us (8%)
  blocking collectives  37 us (7%)
  between operations  13.7 us (3%)
  starting transfers between devices  12 us (2%)
    all_gather x1, waiting for transfers between devices, on_device(): lax.all_gather(w_inner, 'seq', axis=0, tiled=True)  111 us
    ppermute x9, waiting for transfers between devices, passed_along(): return lax.ppermute(value, axis, pairs)  98.4 us
    reduce_scatter x1, waiting for transfers between devices, on_device(): lax.psum_scatter(partial_out, 'tp', scatter_dimension=1, tiled=True)  75.3 us
    all_gather x1, waiting for transfers between devices, on_device(): whole = lax.all_gather(tokens, 'tp', axis=1, tiled=True)  37 us
    all_gather x1, blocking collectives, on_device(): lax.all_gather(w_step, 'seq', axis=0, tiled=True)  30.9 us
    reshape x2, local copies, waits for them, and re-layouts, on_device(): (y_inner + y_carry).reshape(row_count, inner_here)  15.8 us
    reduce_sum x1, other arithmetic, on_device(): squares = lax.psum(jnp.sum(gated * gated, axis=1), 'tp')  15.2 us
    unnamed x69, local copies, waits for them, and re-layouts  14 us
  transfers between devices with their start and end apart: 14, of which 12 were waited for; matrix products, arithmetic and copies ran while one was open for 25% of the time, Pallas kernels for 0%

commit v1 on v0

--- a/solution.py
+++ b/solution.py
@@ -117,10 +117,17 @@
         fold_block, (unit_gain, zero_state), (block_gain_each, fresh)
     )
 
-    def relay(iteration, entering_now):
-        return passed_along(block_gain[:, None, None] * entering_now + block_state, "seq", 1)
-
-    entering = lax.fori_loop(0, lax.axis_size("seq") - 1, relay, zero_state)
+    seq_count = lax.axis_size("seq")
+    reach = min(seq_count - 1, -(-(total_blocks // 2) // local_blocks))
+    gains = lax.all_gather(block_gain, "seq", axis=0)
+    sent_state = block_state.astype(jnp.bfloat16)
+    entering = zero_state
+    factor = unit_gain
+    for distance in range(1, reach + 1):
+        arrived = passed_along(sent_state, "seq", distance)
+        entering = entering + factor[:, None, None] * arrived.astype(jnp.float32)
+        source = jnp.maximum(seq_index - distance, 0)
+        factor = factor * lax.dynamic_index_in_dim(gains, source, 0, keepdims=False)
 
     def pass_block(previous, item):
         log_now, keep_now, fresh_now = item
@@ -138,13 +145,15 @@
     gated = y_total * jax.nn.silu(gate_in.astype(jnp.float32))
     squares = lax.psum(jnp.sum(gated * gated, axis=1), "tp")
     square_mean = squares / (inner_here * lax.axis_size("tp"))
-    normed = (gated * lax.rsqrt(square_mean + 1e-05)[:, None] * norm_gain).astype(jnp.bfloat16)
+    normed = (gated * norm_gain).astype(jnp.bfloat16)
     partial_out = jnp.dot(
         normed,
         lax.all_gather(w_output, "seq", axis=1, tiled=True),
         preferred_element_type=jnp.float32,
     )
-    summed = lax.psum_scatter(partial_out, "tp", scatter_dimension=1, tiled=True)
+    summed = lax.psum_scatter(
+        partial_out.astype(jnp.bfloat16), "tp", scatter_dimension=1, tiled=True
+    ).astype(jnp.float32) * lax.rsqrt(square_mean + 1e-05)[:, None]
     live = in_block < jnp.repeat(local_valid, BLOCK)
     return jnp.where(live[:, None], summed, 0.0).astype(jnp.bfloat16)
 

time: 545 us -> 492 us (0.903)
  waiting for transfers between devices: 326 us -> 193 us
  blocking collectives: 37 us -> 116 us
    ppermute x9 -> x6, waiting for transfers between devices: 98.4 us -> 2.25 us  [passed_along(): return lax.ppermute(value, axis, pairs)]
    unnamed x0 -> x1, blocking collectives: none -> 79.3 us
    reduce_scatter x1, waiting for transfers between devices: 75.3 us -> 39.1 us  [on_device(): lax.psum_scatter(partial_out.astype(jnp.bfloat16), 'tp', scatter_dimensio...]
    ppermute x9 -> x6, starting transfers between devices: 11.8 us -> 7.92 us  [passed_along(): return lax.ppermute(value, axis, pairs)]
    unnamed x69 -> x70, local copies, waits for them, and re-layouts: 14 us -> 17 us
  transfers between devices with their start and end apart: 14 -> 11, of which waited for: 12 -> 5; matrix products, arithmetic and copies ran while one was open for 25% -> 29% of each run, Pallas kernels for 0% -> 0%
where the time goes in v1:
time: 492 us; the launch traced here: 488 us
  waiting for transfers between devices  193 us (39%)
  blocking collectives  116 us (24%)
  other arithmetic  58.7 us (12%)
  local copies, waits for them, and re-layouts  53.9 us (11%)
  matrix products  44.5 us (9%)
  between operations  14.3 us (3%)
  starting transfers between devices  8.08 us (2%)
    all_gather x1, waiting for transfers between devices, on_device(): lax.all_gather(w_inner, 'seq', axis=0, tiled=True)  111 us
    unnamed x1, blocking collectives  79.3 us
    reduce_scatter x1, waiting for transfers between devices, on_device(): lax.psum_scatter(partial_out.astype(jnp.bfloat16), 'tp', scatter_dimensio...  39.1 us
    all_gather x1, waiting for transfers between devices, on_device(): whole = lax.all_gather(tokens, 'tp', axis=1, tiled=True)  37 us
    all_gather x1, blocking collectives, on_device(): lax.all_gather(w_step, 'seq', axis=0, tiled=True)  30.9 us
    unnamed x70, local copies, waits for them, and re-layouts  17 us
    reshape x2, local copies, waits for them, and re-layouts, on_device(): (y_inner + y_carry).reshape(row_count, inner_here)  15.8 us
    reduce_sum x1, other arithmetic, on_device(): squares = lax.psum(jnp.sum(gated * gated, axis=1), 'tp')  15.1 us
  transfers between devices with their start and end apart: 11, of which 5 were waited for; matrix products, arithmetic and copies ran while one was open for 29% of the time, Pallas kernels for 0%

profile of v1, /device:TPU:26, one launch (start us, length us, event | category | flops | bytes accessed | tf_op | source)
XLA Modules:
  0.0 488.2 jit_solution(9168531050138183106)
XLA Ops:
  13.5 30.9 %all_gather.23 = bf16[2048,16]{0,1:T(8,128)(2,1)S(1)} all-gather(bf16[256,16]{0,1:T(8,128)(2,1)} %param.20), channel_id=1, replica_groups=mesh['seq'=8,'tp'=4] {'seq'}, dimensions={0}, use_global_device_ids=true | all-gather | bytes 73728 | tf_op jit(solution)/shard_map/all_gather | solution.py:68
  48.7 37.0 %all-gather.6.cloned.1.call-done = bf16[1024,2048]{1,0:T(8,128)(2,1)} async-done(((bf16[1024,512]{1,0:T(8,128)(2,1)}), bf16[1024,2048]{1,0:T(8,128)(2,1)}) %all-gather.6.cloned.1.call-update) | async-done | bytes 4194320 | tf_op jit(solution)/shard_map/all_gather | solution.py:64
  85.7 3.9 convolution_convert_fusion.2
  92.2 2.3 reduce-window.6
  98.5 111.4 %all-gather.8.cloned.1.call-done = bf16[2048,2,1024]{2,1,0:T(2,128)(2,1)} async-done(((bf16[256,2,1024]{2,1,0:T(2,128)(2,1)}), bf16[2048,2,1024]{2,1,0:T(2,128)(2,1)}) %all-gather.8.cloned.1.call-update) | async-done | bytes 8388624 | tf_op jit(solution)/shard_map/all_gather | solution.py:66
  209.9 10.2 %copy.98 = bf16[256,8,2,1024]{3,1,2,0:T(8,128)(2,1)} copy(bf16[256,8,2,1024]{3,2,1,0:T(2,128)(2,1)} %bitcast.106) | data formatting | bytes 16777216
  220.1 12.9 %convolution_convert_fusion = bf16[1024,2048]{1,0:T(8,128)(2,1)S(1)} fusion(bf16[1024,2048]{1,0:T(8,128)(2,1)} %all-gather.6.cloned.1.call-done, bf16[2048,2048]{1,0:T(8,128)(2,1)} %bitcast.107), kind=kOutput, calls=%fused_computation.43 | convolution fusion | flops 8592031744 | bytes 16777216 | tf_op jit(solution)/shard_map/dot_general | solution.py:71
  236.3 2.2 collective-permute-done
  241.2 4.0 multiply_convert_fusion.5
  245.2 4.0 reshape.163
  249.1 4.9 %copy.80 = bf16[4,256,16,64]{1,3,2,0:T(8,128)(2,1)S(1)} copy(bf16[4,256,16,64]{3,2,1,0:T(8,128)(2,1)} %reshape.163) | data formatting | bytes 4194304 | tf_op jit(solution)/shard_map/reshape | solution.py:88
  254.0 7.4 %fusion.14 = f32[4,16,128,64]{3,2,1,0:T(8,128)} fusion(bf16[4,256,16,64]{1,3,2,0:T(8,128)(2,1)S(1)} %copy.80, f32[4,256,128]{2,1,0:T(8,128)} %convert_element_type.86, f32[4,256,16]{1,2,0:T(8,128)S(1)} %get-tuple-element.173), kind=kOutput, calls=%fused_computation.25 | convolution fusion | flops 272629760 | bytes 4784128 | tf_op jit(solution)/shard_map/cjhn,cjhp->chnp/dot_general | solution.py:106
  261.4 10.6 %while.26 = (s32[]{:T(128)}, f32[16]{0:T(128)}, f32[16,128,64]{2,1,0:T(8,128)S(1)}, f32[4,16]{1,0:T(4,128)}, f32[4,16,128,64]{3,2,1,0:T(8,128)}, /*index=5*/s32[]{:T(128)}, s32[]{:T(128)}) while((s32[]{:T(128)}, f32[16]{0:T(128)}, f32[16,128,64]{2,1,0:T(8,128)S(1)}, f32[4,16]{1,0:T(4,128)}, f32[4,16,128,64]{3,2,1,0:T(8,128)}, ...), condition=%wide.region_5.6_spmd.clone, body=%wide.region_4.5_spmd.clone.sunk | while | flops 393251 | bytes 1573280 | solution.py:116
  278.2 2.2 fusion.61
  281.2 79.3 %all-reduce = f32[128]{0:T(128)S(1)} all-reduce(f32[128]{0:T(128)S(1)} %dynamic-update-slice), channel_id=2, replica_groups=mesh['seq'=8,'tp'=4] {'seq'}, use_global_device_ids=true, to_apply=%add | all-reduce | flops 128 | bytes 1024
  363.6 19.4 %while.25 = (s32[]{:T(128)}, f32[16,128,64]{2,1,0:T(8,128)S(1)}, bf16[4,16,128,64]{3,2,1,0:T(8,128)(2,1)}, f32[4,16]{1,0:T(4,128)}, f32[4]{0:T(128)S(1)}, /*index=5*/f32[4,16,128,64]{3,2,1,0:T(8,128)}, s32[]{:T(128)}) while((s32[]{:T(128)}, f32[16,128,64]{2,1,0:T(8,128)S(1)}, bf16[4,16,128,64]{3,2,1,0:T(8,128)(2,1)}, f32[4,16]{1,0:T(4,128)}, ...), condition=%wide.region_7.8_spmd, body=%wide.region_6.7_spmd.sunk | while | flops 524290 | bytes 3147045 | solution.py:137
  386.3 6.2 %bitcast_add_fusion.2 = f32[4,256,16,64]{1,3,2,0:T(8,128)} fusion(f32[4,256,16,64]{1,3,2,0:T(8,128)S(1)} %bitcast.108, bf16[4,256,16,64]{1,3,2,0:T(8,128)(2,1)S(1)} %copy.80, f32[4,256,16]{1,2,0:T(8,128)S(1)} %bitcast.117, f32[4,256,256]{2,1,0:T(8,128)S(1)} %copy-done.4, f32[4,256,16]{1,2,0:T(8,128)S(1)} %bitcast_bitcast_fusion, ...), kind=kOutput, calls=%fused_computation.37 | convolution fusion | flops 559939584 | bytes 11796480 | tf_op jit(solution)/shard_map/cijh,cjhp->cihp/dot_general | solution.py:100
  392.5 8.1 %copy.89 = f32[4,256,16,64]{3,2,1,0:T(8,128)} copy(f32[4,256,16,64]{1,3,2,0:T(8,128)} %bitcast_add_fusion.2) | data formatting | bytes 8388608 | tf_op jit(solution)/shard_map/reshape | solution.py:142
  400.7 7.7 %reshape.162 = f32[1024,1024]{1,0:T(8,128)} reshape(f32[4,256,16,64]{3,2,1,0:T(8,128)} %copy.89) | data formatting | bytes 8388608 | tf_op jit(solution)/shard_map/reshape | solution.py:142
  408.4 15.1 %multiply_reduce_fusion = (f32[1024]{0:T(1024)S(1)}, f32[1024,1024]{1,0:T(8,128)}) fusion(bf16[1024,2048]{1,0:T(8,128)(2,1)} %copy-done.2, f32[1024,1024]{1,0:T(8,128)} %reshape.162, f32[1024]{0:T(1024)S(1)} %copy-done.23, f32[1024]{0:T(1024)S(1)} %bitcast.123, f32[1027,1024]{1,0:T(8,128)} %copy-done, pred[1024]{0:T(1024)(128)(4,1)S(1)} %copy-done.16, ...), kind=kLoop, calls=%fused_computation.38 | loop fusion | flops 28310528 | bytes 27291648 | tf_op jit(solution)/shard_map/reduce_sum | solution.py:146
  423.5 10.0 %convolution_convert_fusion.1 = bf16[1024,2048]{1,0:T(8,128)(2,1)} fusion(bf16[1024,2048]{1,0:T(8,128)(2,1)} %all-gather.12.cloned.1.call-done, f32[1024,1024]{1,0:T(8,128)} %get-tuple-element.166, f32[1024]{0:T(1024)S(1)} %copy-done.27), kind=kOutput, calls=%fused_computation.44 | convolution fusion | flops 4299161600 | bytes 12587008 | tf_op jit(solution)/shard_map/dot_general | solution.py:149
  434.4 5.7 %psum.7 = f32[1024]{0:T(1024)S(1)} all-reduce(f32[1024]{0:T(1024)S(1)} %get-tuple-element.165), channel_id=1, replica_groups=mesh['seq'=8,'tp'=4] {'tp'}, use_global_device_ids=true, to_apply=%region_10.11 | all-reduce | flops 1024 | bytes 8192 | tf_op jit(solution)/shard_map/psum | solution.py:146
  440.1 39.1 %reduce-scatter.2.cloned.1.call-done = bf16[1024,512]{1,0:T(8,128)(2,1)} async-done(((bf16[1024,2048]{1,0:T(8,128)(2,1)}), bf16[1024,512]{1,0:T(8,128)(2,1)}) %reduce-scatter.2.cloned.1.call-update) | async-done | bytes 1048592 | tf_op jit(solution)/shard_map/reduce_scatter | solution.py:154
  479.2 2.5 select_convert_fusion
  (163 shorter events, 66.9 us)
Async XLA Ops:
  6.5 42.2 %all-gather.10.cloned.1.call-start = ((), (), s32[]{:S(2)}) async-start(), calls=%async_computation.3 | async-start | bytes 1179648 | tf_op jit(solution)/shard_map/all_gather | solution.py:67
  7.3 78.5 %all-gather.6.cloned.1.call-start = ((), (), s32[]{:S(2)}) async-start(), calls=%async_computation.1 | async-start | bytes 5242880 | tf_op jit(solution)/shard_map/all_gather | solution.py:64
  8.0 201.9 %all-gather.8.cloned.1.call-start = ((), (), s32[]{:S(2)}) async-start(), calls=%async_computation.2 | async-start | bytes 9437184 | tf_op jit(solution)/shard_map/all_gather | solution.py:66
  8.7 82.2 %copy-start.24 = (f32[16]{0:T(128)S(1)}, f32[16]{0:T(128)}, u32[]{:S(2)}) copy-start(f32[16]{0:T(128)} %param.24) | copy-start | bytes 196
  8.8 414.7 %all-gather.12.cloned.1.call-start = ((), (), s32[]{:S(2)}) async-start(), calls=%async_computation.4 | async-start | bytes 4718592 | tf_op jit(solution)/shard_map/all_gather | solution.py:151
  9.3 469.8 %reduce-scatter.2.cloned.1.call-start = ((), (), s32[]{:S(2)}) async-start(), calls=%async_computation.5 | async-start | bytes 5242880 | tf_op jit(solution)/shard_map/reduce_scatter | solution.py:154
  11.0 84.7 %copy-start.25 = (f32[4]{0:T(128)}, f32[4]{0:T(128)S(1)}, u32[]{:S(2)}) copy-start(f32[4]{0:T(128)S(1)} %compare_select_fusion.1) | copy-start | bytes 52
  11.8 85.3 %copy-start.11 = (pred[1024]{0:T(1024)(128)(4,1)}, pred[1024]{0:T(1024)(128)(4,1)S(1)}, u32[]{:S(2)}) copy-start(pred[1024]{0:T(1024)(128)(4,1)S(1)} %get-tuple-element.182) | copy-start | bytes 3076
  11.8 85.3 %copy-start.14 = (pred[1024]{0:T(1024)(128)(4,1)}, pred[1024]{0:T(1024)(128)(4,1)S(1)}, u32[]{:S(2)}) copy-start(pred[1024]{0:T(1024)(128)(4,1)S(1)} %get-tuple-element.183) | copy-start | bytes 3076
  11.8 85.3 %copy-start.17 = (pred[1024]{0:T(1024)(128)(4,1)}, pred[1024]{0:T(1024)(128)(4,1)S(1)}, u32[]{:S(2)}) copy-start(pred[1024]{0:T(1024)(128)(4,1)S(1)} %get-tuple-element.184) | copy-start | bytes 3076
  11.8 85.3 %copy-start.20 = (pred[1024]{0:T(1024)(128)(4,1)}, pred[1024]{0:T(1024)(128)(4,1)S(1)}, u32[]{:S(2)}) copy-start(pred[1024]{0:T(1024)(128)(4,1)S(1)} %get-tuple-element.185) | copy-start | bytes 3076
  89.6 7.3 %collective-permute-start.1 = (bf16[3,256]{1,0:T(4,128)(2,1)S(1)}, bf16[3,256]{1,0:T(4,128)(2,1)S(1)}, u32[]{:S(2)}, u32[]{:S(2)}) collective-permute-start(bf16[3,256]{1,0:T(4,128)(2,1)S(1)} %slice.109), channel_id=1, source_target_pairs={{0,4},{4,8},{8,12},{12,16},{16,20},{20,24},{24,28},{1,5},{5,9},{9,... | collective-permute-start | bytes 4616 | tf_op jit(solution)/shard_map/ppermute | solution.py:12
  95.0 125.1 %copy-start.10 = (f32[4,16]{1,0:T(4,128)}, f32[4,16]{1,0:T(4,128)S(1)}, u32[]{:S(2)}) copy-start(f32[4,16]{1,0:T(4,128)S(1)} %slice_reduce_fusion) | copy-start | bytes 772
  233.0 5.5 %collective-permute-start = (bf16[3,1024]{1,0:T(4,128)(2,1)S(1)}, bf16[3,1024]{1,0:T(4,128)(2,1)S(1)}, u32[]{:S(2)}, u32[]{:S(2)}) collective-permute-start(bf16[3,1024]{1,0:T(4,128)(2,1)S(1)} %slice.101), channel_id=1, source_target_pairs={{0,4},{4,8},{8,12},{12,16},{16,20},{20,24},{24,28},{1,5},{5,9},{9,... | collective-permute-start | bytes 18440 | tf_op jit(solution)/shard_map/ppermute | solution.py:12
  272.0 91.6 %copy-start.26 = (f32[4]{0:T(128)S(1)}, f32[4]{0:T(128)}, u32[]{:S(2)}) copy-start(f32[4]{0:T(128)} %copy-done.25) | copy-start | bytes 52
  273.0 87.7 %collective-permute-start.2 = (bf16[16,128,64]{2,1,0:T(8,128)(2,1)}, bf16[16,128,64]{2,1,0:T(8,128)(2,1)S(1)}, u32[]{:S(2)}, u32[]{:S(2)}) collective-permute-start(bf16[16,128,64]{2,1,0:T(8,128)(2,1)} %convert_element_type.88), channel_id=1, source_target_pairs={{0,4},{4,8},{8,12},{12,16},{16,20},{20,24},{24,28},{1,5},{5,9},{9,... | collective-permute-start | bytes 786440 | tf_op jit(solution)/shard_map/ppermute | solution.py:12
  274.3 86.4 %collective-permute-start.3 = (bf16[16,128,64]{2,1,0:T(8,128)(2,1)}, bf16[16,128,64]{2,1,0:T(8,128)(2,1)S(1)}, u32[]{:S(2)}, u32[]{:S(2)}) collective-permute-start(bf16[16,128,64]{2,1,0:T(8,128)(2,1)} %convert_element_type.88), channel_id=1, source_target_pairs={{0,8},{4,12},{8,16},{12,20},{16,24},{20,28},{1,9},{5,13},{9,17},{1... | collective-permute-start | bytes 786440 | tf_op jit(solution)/shard_map/ppermute | solution.py:12
  275.6 85.1 %collective-permute-start.4 = (bf16[16,128,64]{2,1,0:T(8,128)(2,1)}, bf16[16,128,64]{2,1,0:T(8,128)(2,1)}, u32[]{:S(2)}, u32[]{:S(2)}) collective-permute-start(bf16[16,128,64]{2,1,0:T(8,128)(2,1)} %convert_element_type.88), channel_id=1, source_target_pairs={{0,12},{4,16},{8,20},{12,24},{16,28},{1,13},{5,17},{9,21},{13,25},... | collective-permute-start | bytes 786440 | tf_op jit(solution)/shard_map/ppermute | solution.py:12
  276.9 83.8 %collective-permute-start.5 = (bf16[16,128,64]{2,1,0:T(8,128)(2,1)}, bf16[16,128,64]{2,1,0:T(8,128)(2,1)}, u32[]{:S(2)}, u32[]{:S(2)}) collective-permute-start(bf16[16,128,64]{2,1,0:T(8,128)(2,1)} %convert_element_type.88), channel_id=1, source_target_pairs={{0,16},{4,20},{8,24},{12,28},{1,17},{5,21},{9,25},{13,29},{2,18},{... | collective-permute-start | bytes 786440 | tf_op jit(solution)/shard_map/ppermute | solution.py:12
  363.6 21.5 %copy-start.3 = (bf16[1024,128]{1,0:T(8,128)(2,1)S(1)}, bf16[1024,128]{1,0:T(8,128)(2,1)}, u32[]{:S(2)}) copy-start(bf16[1024,128]{1,0:T(8,128)(2,1)} %get-tuple-element.171) | copy-start | bytes 786436
  400.7 7.7 %copy-start.19 = (pred[1024]{0:T(1024)(128)(4,1)S(1)}, pred[1024]{0:T(1024)(128)(4,1)}, u32[]{:S(2)}) copy-start(pred[1024]{0:T(1024)(128)(4,1)} %copy-done.17) | copy-start | bytes 3076
  400.7 7.7 %copy-start.22 = (pred[1024]{0:T(1024)(128)(4,1)S(1)}, pred[1024]{0:T(1024)(128)(4,1)}, u32[]{:S(2)}) copy-start(pred[1024]{0:T(1024)(128)(4,1)} %copy-done.20) | copy-start | bytes 3076
  400.7 7.7 %copy-start.23 = (f32[1024]{0:T(1024)S(1)}, f32[1024]{0:T(1024)}, u32[]{:S(2)}) copy-start(f32[1024]{0:T(1024)} %mul.309) | copy-start | bytes 12292
  408.4 15.1 %copy-start.27 = (f32[1024]{0:T(1024)S(1)}, f32[1024]{0:T(1024)}, u32[]{:S(2)}) copy-start(f32[1024]{0:T(1024)} %param.26) | copy-start | bytes 12292
  (19 other events, 59.4 us)
Sparse Core Ops, SparseCore 0:
  9.5 39.1 all-gather.9
  50.3 35.4 all-gather.5
  87.9 121.9 all-gather.7
  211.8 77.8 all-gather.11
  433.6 45.5 reduce-scatter.1

commit v2 on v0

v2 whole, which is shorter than its diff:
```python
import functools

import jax
import jax.numpy as jnp
from jax import lax
from jax.experimental import pallas as pl
from jax.experimental.pallas import tpu as pltpu
from jax.sharding import PartitionSpec as P

BLOCK = 256


def passed_along(value, axis, by):
    count = lax.axis_size(axis)
    pairs = [(i, i + by) for i in range(count) if 0 <= i + by < count]
    return lax.ppermute(value, axis, pairs)


def convolve(values, edge_rows, weights, in_block, carry_on):
    lag_rows = weights.shape[0] - 1
    row_total = values.shape[0]
    widened = jnp.concatenate([edge_rows, values], axis=0).astype(jnp.float32)
    total = jnp.zeros(values.shape, jnp.float32)
    for offset in range(weights.shape[0]):
        shifted = widened[lag_rows - offset : lag_rows - offset + row_total]
        keeping = (in_block >= offset) | carry_on
        total = total + jnp.where(keeping[:, None], shifted, 0.0) * weights[offset]
    return jax.nn.silu(total).astype(jnp.bfloat16)


LANES = 128
ROW_CHUNK = 256
VMEM_BYTES = 50 * 1024 * 1024


def spread_heads(columns, tile, head_size):
    per_tile = LANES // head_size
    lane = lax.broadcasted_iota(jnp.int32, (columns.shape[0], LANES), 1)
    result = columns[:, tile * per_tile : tile * per_tile + 1]
    for k in range(1, per_tile):
        head = tile * per_tile + k
        result = jnp.where(lane < k * head_size, result, columns[:, head : head + 1])
    return result


def state_kernel(head_size, x_ref, bc_ref, cum_ref, step_ref, gain_ref, fresh_ref, total_ref):
    block = pl.program_id(0)
    state_size = bc_ref.shape[1] // 2

    @pl.when(block == 0)
    def _():
        total_ref[...] = jnp.zeros_like(total_ref)

    cum = cum_ref[...]
    tail = jnp.exp(cum[BLOCK - 1 : BLOCK, :] - cum) * step_ref[...]
    b_rows = bc_ref[:, :state_size]
    for tile in range(x_ref.shape[1] // LANES):
        cols = slice(tile * LANES, (tile + 1) * LANES)
        weighted = x_ref[:, cols].astype(jnp.float32) * spread_heads(tail, tile, head_size)
        fresh = lax.dot_general(
            b_rows,
            weighted.astype(jnp.bfloat16),
            (((0,), (0,)), ((), ())),
            preferred_element_type=jnp.float32,
        )
        fresh_ref[0, :, cols] = fresh
        total_ref[:, cols] = total_ref[:, cols] * gain_ref[0, :, cols] + fresh


def mix_kernel(
    head_size,
    x_ref,
    bc_ref,
    gate_ref,
    cum_ref,
    cum_t_ref,
    step_t_ref,
    gain_ref,
    keep_ref,
    fresh_ref,
    entering_ref,
    skip_ref,
    norm_ref,
    out_ref,
    square_ref,
    state_ref,
):
    block = pl.program_id(0)
    state_size = bc_ref.shape[1] // 2
    per_tile = LANES // head_size

    @pl.when(block == 0)
    def _():
        state_ref[...] = entering_ref[...]

    b_rows = bc_ref[:, :state_size]
    c_rows = bc_ref[:, state_size:]
    products = lax.dot_general(
        c_rows, b_rows, (((1,), (1,)), ((), ())), preferred_element_type=jnp.float32
    )
    rows = lax.broadcasted_iota(jnp.int32, (BLOCK, BLOCK), 0)
    causal = rows >= lax.broadcasted_iota(jnp.int32, (BLOCK, BLOCK), 1)
    lane = lax.broadcasted_iota(jnp.int32, (BLOCK, LANES), 1)
    cum = cum_ref[...]
    grown = jnp.exp(cum)
    squares = jnp.zeros((BLOCK, LANES), jnp.float32)
    for tile in range(x_ref.shape[1] // LANES):
        cols = slice(tile * LANES, (tile + 1) * LANES)
        x_tile = x_ref[:, cols]
        y_tile = None
        for k in range(per_tile):
            head = tile * per_tile + k
            spread = cum[:, head : head + 1] - cum_t_ref[head : head + 1, :]
            decays = jnp.exp(jnp.where(causal, spread, -jnp.inf))
            mixing = decays * products * step_t_ref[head : head + 1, :]
            part = jnp.dot(
                mixing.astype(jnp.bfloat16), x_tile, preferred_element_type=jnp.float32
            )
            y_tile = part if k == 0 else jnp.where(lane < k * head_size, y_tile, part)
        previous = state_ref[:, cols]
        incoming = (previous * keep_ref[0, :, cols]).astype(jnp.bfloat16)
        carried = jnp.dot(c_rows, incoming, preferred_element_type=jnp.float32)
        state_ref[:, cols] = previous * gain_ref[0, :, cols] + fresh_ref[0, :, cols]
        y_tile = y_tile + spread_heads(grown, tile, head_size) * carried
        y_tile = y_tile + skip_ref[:, cols] * x_tile.astype(jnp.float32)
        gate = gate_ref[:, cols].astype(jnp.float32)
        gated = y_tile * (gate * jax.nn.sigmoid(gate))
        squares = squares + gated * gated
        out_ref[:, cols] = (gated * norm_ref[:, cols]).astype(jnp.bfloat16)
    square_ref[...] = jnp.sum(squares, axis=1, keepdims=True)


def output_kernel(
    tp_count, a_ref, w_ref, out_ref, send_a, recv_a, send_b, recv_b, sa_sem, ra_sem, sb_sem, rb_sem
):
    mesh_id = pl.DeviceIdType.MESH
    chips = tp_count // 2
    width = out_ref.shape[1]
    chunks = out_ref.shape[0] // ROW_CHUNK
    me = lax.axis_index("tp")
    chip = me // 2
    core = lax.rem(me, 2)
    partner = chip * 2 + (1 - core)

    def chip_at(offset):
        return lax.rem(chip + offset, chips)

    barrier = pltpu.get_barrier_semaphore()
    pl.semaphore_signal(barrier, inc=1, device_id={"tp": partner}, device_id_type=mesh_id)
    for offset in range(1, chips):
        pl.semaphore_signal(
            barrier,
            inc=1,
            device_id={"tp": chip_at(offset) * 2 + core},
            device_id_type=mesh_id,
        )
    pl.semaphore_wait(barrier, chips)

    def product(chunk, owner):
        columns = pl.ds(pl.multiple_of(owner * width, LANES), width)
        return jnp.dot(
            a_ref[chunk * ROW_CHUNK : (chunk + 1) * ROW_CHUNK, :],
            w_ref[:, columns],
            preferred_element_type=jnp.float32,
        )

    def to_partner(chunk, offset):
        return pltpu.make_async_remote_copy(
            src_ref=send_a.at[chunk, offset],
            dst_ref=recv_a.at[chunk, offset],
            send_sem=sa_sem.at[chunk, offset],
            recv_sem=ra_sem.at[chunk, offset],
            device_id={"tp": partner},
            device_id_type=mesh_id,
        )

    def to_chip(chunk, offset):
        return pltpu.make_async_remote_copy(
            src_ref=send_b.at[chunk, offset - 1],
            dst_ref=recv_b.at[chunk, offset - 1],
            send_sem=sb_sem.at[chunk, offset - 1],
            recv_sem=rb_sem.at[chunk, offset - 1],
            device_id={"tp": chip_at(offset) * 2 + core},
            device_id_type=mesh_id,
        )

    def first_half(chunk, offset):
        send_a[chunk, offset] = product(chunk, chip_at(offset) * 2 + 1 - core).astype(jnp.bfloat16)
        to_partner(chunk, offset).start()

    def second_half(chunk, offset):
        own = product(chunk, chip_at(offset) * 2 + core)
        to_partner(chunk, offset).wait()
        send_b[chunk, offset - 1] = (own + recv_a[chunk, offset].astype(jnp.float32)).astype(
            jnp.bfloat16
        )
        to_chip(chunk, offset).start()

    for chunk in range(chunks):
        for offset in range(1, chips):
            first_half(chunk, offset)
            if chunk > 0:
                second_half(chunk - 1, offset)
    for offset in range(1, chips):
        second_half(chunks - 1, offset)
    for chunk in range(chunks):
        first_half(chunk, 0)
    for chunk in range(chunks):
        own = product(chunk, me)
        to_partner(chunk, 0).wait()
        total = own + recv_a[chunk, 0].astype(jnp.float32)
        for offset in range(1, chips):
            to_chip(chunk, offset).wait()
            total = total + recv_b[chunk, offset - 1].astype(jnp.float32)
        out_ref[chunk * ROW_CHUNK : (chunk + 1) * ROW_CHUNK, :] = total


def projected_sum(rows, weights, tp_count):
    row_count, width = rows.shape[0], weights.shape[1] // tp_count
    chunks, chips = row_count // ROW_CHUNK, tp_count // 2
    vmem = pl.BlockSpec(memory_space=pltpu.VMEM)
    return pl.pallas_call(
        functools.partial(output_kernel, tp_count),
        out_shape=jax.ShapeDtypeStruct((row_count, width), jnp.float32),
        in_specs=[vmem, vmem],
        out_specs=vmem,
        scratch_shapes=[
            pltpu.VMEM((chunks, chips, ROW_CHUNK, width), jnp.bfloat16),
            pltpu.VMEM((chunks, chips, ROW_CHUNK, width), jnp.bfloat16),
            pltpu.VMEM((chunks, chips - 1, ROW_CHUNK, width), jnp.bfloat16),
            pltpu.VMEM((chunks, chips - 1, ROW_CHUNK, width), jnp.bfloat16),
            pltpu.SemaphoreType.DMA((chunks, chips)),
            pltpu.SemaphoreType.DMA((chunks, chips)),
            pltpu.SemaphoreType.DMA((chunks, chips - 1)),
            pltpu.SemaphoreType.DMA((chunks, chips - 1)),
        ],
        compiler_params=pltpu.CompilerParams(
            collective_id=3, has_side_effects=True, vmem_limit_bytes=VMEM_BYTES
        ),
        name="output_kernel",
    )(rows, weights)


def on_device(
    tokens,
    w_inner,
    w_states,
    w_step,
    conv_inner,
    conv_states,
    decay_rate,
    step_bias,
    skip_gain,
    norm_gain,
    w_output,
    block_owner,
    lengths,
):
    row_count = tokens.shape[0]
    local_blocks = row_count // BLOCK
    total_blocks = block_owner.shape[0]
    heads_here = w_step.shape[1]
    inner_here = w_inner.shape[2]
    state_size = w_states.shape[1] // 2
    head_size = inner_here // heads_here
    lag_rows = conv_inner.shape[0] - 1
    block_ids = jnp.arange(total_blocks, dtype=jnp.int32)
    same_owner = block_owner[:, None] == block_owner[None, :]
    first_block = jnp.min(jnp.where(same_owner, block_ids[None, :], total_blocks), axis=1)
    starting = (first_block == block_ids).astype(jnp.int32)
    request_ids = jnp.arange(lengths.shape[0], dtype=jnp.int32)
    own_length = jnp.sum(
        jnp.where(block_owner[:, None] == request_ids[None, :], lengths[None, :], 0), axis=1
    )
    valid_rows = jnp.clip(own_length - (block_ids - first_block) * BLOCK, 0, BLOCK)
    seq_index = lax.axis_index("seq")
    local_start = lax.dynamic_slice_in_dim(starting, seq_index * local_blocks, local_blocks)
    local_valid = lax.dynamic_slice_in_dim(valid_rows, seq_index * local_blocks, local_blocks)
    in_block = jnp.arange(row_count, dtype=jnp.int32) % BLOCK
    carry_on = jnp.repeat(local_start == 0, BLOCK)
    whole = lax.all_gather(tokens, "tp", axis=1, tiled=True)
    shard = jnp.concatenate(
        [w_inner.reshape(w_inner.shape[0], 2 * inner_here), w_states, w_step], axis=1
    )
    weights = lax.all_gather(shard, "seq", axis=0, tiled=True)
    projected = jnp.dot(whole, weights, preferred_element_type=jnp.float32).astype(jnp.bfloat16)
    states_end = 2 * inner_here + 2 * state_size
    x_in = projected[:, inner_here : 2 * inner_here]
    bc_in = projected[:, 2 * inner_here : states_end]
    step_raw = projected[:, states_end:]
    edges = passed_along(projected[row_count - lag_rows :, inner_here:states_end], "seq", 1)
    edge_inner, edge_states = edges[:, :inner_here], edges[:, inner_here:]
    x_conv = convolve(x_in, edge_inner, conv_inner, in_block, carry_on)
    bc_conv = convolve(bc_in, edge_states, conv_states, in_block, carry_on)
    step_size = jax.nn.softplus(step_raw.astype(jnp.float32) + step_bias)
    log_decay = -decay_rate * step_size
    cumulative = jnp.cumsum(log_decay.reshape(local_blocks, BLOCK, heads_here), axis=1)
    final_log = cumulative[:, -1, :]
    keep_flag = jnp.where(local_start == 1, 0.0, 1.0).astype(jnp.float32)
    block_gain_each = jnp.exp(final_log) * keep_flag[:, None]
    gain_lanes = jnp.repeat(block_gain_each, head_size, axis=1)[:, None, :]
    keep_lanes = jnp.broadcast_to(keep_flag[:, None, None], gain_lanes.shape)
    cum_rows = cumulative.reshape(row_count, heads_here)
    by_rows = lambda width: pl.BlockSpec((BLOCK, width), lambda c: (c, 0))
    by_block = lambda *dims: pl.BlockSpec((1,) + dims, lambda c: (c, 0, 0))
    fixed = lambda *dims: pl.BlockSpec(dims, lambda c: (0, 0))
    turned = pl.BlockSpec((heads_here, BLOCK), lambda c: (0, c))
    params = pltpu.CompilerParams(vmem_limit_bytes=VMEM_BYTES)
    fresh, block_state = pl.pallas_call(
        functools.partial(state_kernel, head_size),
        grid=(local_blocks,),
        in_specs=[
            by_rows(inner_here),
            by_rows(2 * state_size),
            by_rows(heads_here),
            by_rows(heads_here),
            by_block(1, inner_here),
        ],
        out_specs=[by_block(state_size, inner_here), fixed(state_size, inner_here)],
        out_shape=[
            jax.ShapeDtypeStruct((local_blocks, state_size, inner_here), jnp.float32),
            jax.ShapeDtypeStruct((state_size, inner_here), jnp.float32),
        ],
        compiler_params=params,
        name="state_kernel",
    )(x_conv, bc_conv, cum_rows, step_size, gain_lanes)
    seq_count = lax.axis_size("seq")
    reach = min(seq_count - 1, -(-(total_blocks // 2) // local_blocks))
    device_gain = jnp.prod(gain_lanes, axis=0)
    gain_high = device_gain.astype(jnp.bfloat16)
    gain_low = (device_gain - gain_high.astype(jnp.float32)).astype(jnp.bfloat16)
    message = jnp.concatenate(
        [
            block_state.astype(jnp.bfloat16),
            jnp.broadcast_to(gain_high, (8, inner_here)),
            jnp.broadcast_to(gain_low, (8, inner_here)),
        ],
        axis=0,
    )
    entering = jnp.zeros((state_size, inner_here), jnp.float32)
    factor = jnp.ones((1, inner_here), jnp.float32)
    for distance in range(1, reach + 1):
        arrived = passed_along(message, "seq", distance).astype(jnp.float32)
        entering = entering + factor * arrived[:state_size]
        factor = factor * (
            arrived[state_size : state_size + 1] + arrived[state_size + 8 : state_size + 9]
        )
    normed, squares_here = pl.pallas_call(
        functools.partial(mix_kernel, head_size),
        grid=(local_blocks,),
        in_specs=[
            by_rows(inner_here),
            by_rows(2 * state_size),
            by_rows(inner_here),
            by_rows(heads_here),
            turned,
            turned,
            by_block(1, inner_here),
            by_block(1, inner_here),
            by_block(state_size, inner_here),
            fixed(state_size, inner_here),
            fixed(1, inner_here),
            fixed(1, inner_here),
        ],
        out_specs=[by_rows(inner_here), by_rows(1)],
        out_shape=[
            jax.ShapeDtypeStruct((row_count, inner_here), jnp.bfloat16),
            jax.ShapeDtypeStruct((row_count, 1), jnp.float32),
        ],
        scratch_shapes=[pltpu.VMEM((state_size, inner_here), jnp.float32)],
        compiler_params=params,
        name="mix_kernel",
    )(
        x_conv,
        bc_conv,
        projected,
        cum_rows,
        cum_rows.T,
        step_size.T,
        gain_lanes,
        keep_lanes,
        fresh,
        entering,
        jnp.repeat(skip_gain, head_size)[None, :],
        norm_gain[None, :],
    )
    tp_count = lax.axis_size("tp")
    squares = lax.psum(squares_here[:, 0], "tp")
    square_mean = squares / (inner_here * tp_count)
    summed = projected_sum(normed, lax.all_gather(w_output, "seq", axis=1, tiled=True), tp_count)
    summed = summed * lax.rsqrt(square_mean + 1e-05)[:, None]
    live = in_block < jnp.repeat(local_valid, BLOCK)
    return jnp.where(live[:, None], summed, 0.0).astype(jnp.bfloat16)


def solution(mesh):
    return jax.shard_map(
        on_device,
        mesh=mesh,
        in_specs=(
            P("seq", "tp"),
            P("seq", None, "tp"),
            P("seq", None),
            P("seq", "tp"),
            P(None, "tp"),
            P(),
            P("tp"),
            P("tp"),
            P("tp"),
            P("tp"),
            P("tp", "seq"),
            P(),
            P(),
        ),
        out_specs=P("seq", "tp"),
        check_vma=False,
    )
```

time: 545 us -> 363 us (0.67)
  waiting for transfers between devices: 326 us -> 237 us
  Pallas kernels: 0 us -> 46.8 us
  other arithmetic: 55.4 us -> 16.6 us
  local copies, waits for them, and re-layouts: 51.8 us -> 19.3 us
  blocking collectives: 37 us -> 6.85 us
  matrix products: 45 us -> 15.3 us
    reduce_scatter x1 -> x0, waiting for transfers between devices: 75.3 us -> none  [on_device(): lax.psum_scatter(partial_out, 'tp', scatter_dimension=1, tiled=True)]
    pallas_call x0 -> x3, Pallas kernels: none -> 46.8 us  [the longest x1 30.9 us: projected_sum(): pl.pallas_call(functools.partial(output_kernel, tp_count), out_shape=jax....]
    ppermute x9 -> x5, waiting for transfers between devices: 98.4 us -> 60.7 us  [passed_along(): return lax.ppermute(value, axis, pairs)]
    all_gather x1 -> x0, blocking collectives: 30.9 us -> none  [on_device(): lax.all_gather(w_step, 'seq', axis=0, tiled=True)]
    all_gather x2 -> x1, waiting for transfers between devices: 113 us -> 144 us  [on_device(): weights = lax.all_gather(shard, 'seq', axis=0, tiled=True)]
    dot_general x7 -> x1, matrix products: 44.3 us -> 15.3 us  [on_device(): jnp.dot(whole, weights, preferred_element_type=jnp.float32)]
    reshape x5 -> x3, local copies, waits for them, and re-layouts: 24.7 us -> 0.21 us  [the longest x2 0.2 us: on_device(): cum_rows = cumulative.reshape(row_count, heads_here)]
    reduce_sum x1 -> x0, other arithmetic: 15.2 us -> none  [on_device(): squares = lax.psum(jnp.sum(gated * gated, axis=1), 'tp')]
  transfers between devices with their start and end apart: 14 -> 8, of which waited for: 12 -> 7; matrix products, arithmetic and copies ran while one was open for 25% -> 14% of each run, Pallas kernels for 0% -> 4%
where the time goes in v2:
time: 363 us; the launch traced here: 362 us
  waiting for transfers between devices  237 us (65%)
  Pallas kernels  46.8 us (13%)
  local copies, waits for them, and re-layouts  19.3 us (5%)
  other arithmetic  16.6 us (5%)
  matrix products  15.3 us (4%)
  between operations  13.5 us (4%)
  blocking collectives  6.85 us (2%)
  starting transfers between devices  6.75 us (2%)
    all_gather x1, waiting for transfers between devices, on_device(): weights = lax.all_gather(shard, 'seq', axis=0, tiled=True)  144 us
    ppermute x5, waiting for transfers between devices, passed_along(): return lax.ppermute(value, axis, pairs)  60.7 us
    all_gather x1, waiting for transfers between devices, on_device(): whole = lax.all_gather(tokens, 'tp', axis=1, tiled=True)  31.3 us
    pallas_call x1, Pallas kernels, projected_sum(): pl.pallas_call(functools.partial(output_kernel, tp_count), out_shape=jax....  30.9 us
    dot_general x1, matrix products, on_device(): jnp.dot(whole, weights, preferred_element_type=jnp.float32)  15.3 us
    pallas_call x1, Pallas kernels, on_device(): pl.pallas_call(functools.partial(mix_kernel, head_size), grid=(local_bloc...  10.1 us
    convert_element_type x1, local copies, waits for them, and re-layouts, on_device(): jnp.dot(whole, weights, preferred_element_type=jnp.float32)  7.36 us
  transfers between devices with their start and end apart: 8, of which 7 were waited for; matrix products, arithmetic and copies ran while one was open for 14% of the time, Pallas kernels for 4%

profile of v2, /device:TPU:26, one launch (start us, length us, event | category | flops | bytes accessed | tf_op | source)
XLA Modules:
  0.0 362.2 jit_solution(5581010740218222588)
XLA Ops:
  8.1 1.5 copy.76
  9.6 2.0 pad_maximum_fusion
  13.1 31.3 %all-gather.6.cloned.1.call-done = bf16[1024,2048]{1,0:T(8,128)(2,1)} async-done(((bf16[1024,512]{1,0:T(8,128)(2,1)}), bf16[1024,2048]{1,0:T(8,128)(2,1)}) %all-gather.6.cloned.1.call-update) | async-done | bytes 4194320 | tf_op jit(solution)/shard_map/all_gather | solution.py:281
  44.4 143.7 %all-gather.4.cloned.1.call-done = bf16[2048,2320]{1,0:T(8,128)(2,1)} async-done(((bf16[256,2320]{1,0:T(8,128)(2,1)}), bf16[2048,2320]{1,0:T(8,128)(2,1)}) %all-gather.4.cloned.1.call-update) | async-done | bytes 9502736 | tf_op jit(solution)/shard_map/all_gather | solution.py:285
  188.2 15.3 %fusion = bf16[1024,2320]{0,1:T(8,128)(2,1)S(1)} fusion(bf16[2048,2320]{1,0:T(8,128)(2,1)} %all-gather.4.cloned.1.call-done, bf16[1024,2048]{1,0:T(8,128)(2,1)} %all-gather.6.cloned.1.call-done), kind=kOutput, calls=%fused_computation.1 | convolution fusion | flops 9733160960 | bytes 18448384 | tf_op jit(solution)/shard_map/dot_general | solution.py:286
  203.6 1.5 collective-permute-start
  205.8 2.3 reduce-window.6
  208.8 3.1 slice.146
  212.5 2.7 collective-permute-done
  215.2 2.7 maximum_convert_fusion
  217.9 5.5 %multiply_convert_fusion = bf16[1024,1024]{0,1:T(8,128)(2,1)} fusion(f32[1027,1024]{0,1:T(8,128)S(1)} %maximum_convert_fusion, f32[1024]{0:T(1024)S(1)} %bitcast.60, f32[1024]{0:T(1024)S(1)} %bitcast.61, f32[1024]{0:T(1024)S(1)} %bitcast.59, f32[1024]{0:T(1024)S(1)} %bitcast.58, pred[1024]{0:T(1024)(128)(4,1)S(1)} %get-tuple-element.34, ...), kind=kLoop, calls=%fused_computation.13 | loop fusion | flops 16777216 | bytes 18894848 | tf_op jit(solution)/shard_map/convert_element_type | solution.py:28
  223.4 4.0 %copy.67.x_ref = bf16[1024,1024]{1,0:T(8,128)(2,1)} copy(bf16[1024,1024]{0,1:T(8,128)(2,1)} %multiply_convert_fusion) | data formatting | bytes 4194304 | tf_op jit(solution)/shard_map/convert_element_type | solution.py:28
  229.1 5.9 %state_kernel.1 = (f32[4,128,1024]{2,1,0:T(8,128)}, f32[128,1024]{1,0:T(8,128)S(1)}) custom-call(bf16[1024,1024]{1,0:T(8,128)(2,1)} %copy.67.x_ref, bf16[1024,256]{1,0:T(8,128)(2,1)S(1)} %copy.68.bc_ref, f32[1024,16]{1,0:T(8,128)S(1)} %copy.70.cum_ref, f32[1024,16]{1,0:T(8,128)S(1)} %copy.66.step_ref, f32[4,1,1024]{2,1,0:T(1,128)S(1)} %broadcast_in_dim_reshape.6.gain_ref), custom_call_target="tpu_custom_call" | custom-call | tf_op jit(solution)/shard_map/state_kernel/pallas_call | solution.py:309
  235.0 1.3 collective-permute-start.3
  236.3 1.3 collective-permute-start.2
  237.6 1.3 collective-permute-start.1
  240.5 7.4 %copy.69.gate_ref = bf16[1024,2320]{1,0:T(8,128)(2,1)} copy(bf16[1024,2320]{0,1:T(8,128)(2,1)} %copy-done.1) | data formatting | bytes 9502720 | tf_op jit(solution)/shard_map/convert_element_type | solution.py:286
  247.8 15.7 %collective-permute-done.3 = bf16[144,1024]{1,0:T(8,128)(2,1)S(1)} collective-permute-done((bf16[144,1024]{1,0:T(8,128)(2,1)S(1)}, bf16[144,1024]{1,0:T(8,128)(2,1)S(1)}, u32[]{:S(2)}, u32[]{:S(2)}) %collective-permute-start.3) | collective-permute-done | bytes 294944 | tf_op jit(solution)/shard_map/ppermute | solution.py:16
  263.9 5.6 %collective-permute-done.1 = bf16[144,1024]{1,0:T(8,128)(2,1)S(1)} collective-permute-done((bf16[144,1024]{1,0:T(8,128)(2,1)S(1)}, bf16[144,1024]{1,0:T(8,128)(2,1)S(1)}, u32[]{:S(2)}, u32[]{:S(2)}) %collective-permute-start.1) | collective-permute-done | bytes 294944 | tf_op jit(solution)/shard_map/ppermute | solution.py:16
  269.6 36.4 %collective-permute-done.4 = bf16[144,1024]{1,0:T(8,128)(2,1)S(1)} collective-permute-done((bf16[144,1024]{1,0:T(8,128)(2,1)S(1)}, bf16[144,1024]{1,0:T(8,128)(2,1)S(1)}, u32[]{:S(2)}, u32[]{:S(2)}) %collective-permute-start.4) | collective-permute-done | bytes 294944 | tf_op jit(solution)/shard_map/ppermute | solution.py:16
  306.3 10.1 %mix_kernel.1 = (bf16[1024,1024]{1,0:T(8,128)(2,1)}, f32[1024,1]{1,0:T(8,128)S(1)}) custom-call(bf16[1024,1024]{1,0:T(8,128)(2,1)} %copy.67.x_ref, bf16[1024,256]{1,0:T(8,128)(2,1)S(1)} %copy.68.bc_ref, bf16[1024,2320]{1,0:T(8,128)(2,1)} %copy.69.gate_ref, f32[1024,16]{1,0:T(8,128)S(1)} %copy.70.cum_ref, f32[16,1024]{1,0:T(8,128)S(1)} %bitcast.50, ...), custom_call_target="tpu_custom_call" | custom-call | tf_op jit(solution)/shard_map/mix_kernel/pallas_call | solution.py:348
  316.6 6.9 %psum.7 = f32[1024]{0:T(1024)S(1)} all-reduce(f32[1024]{0:T(1024)S(1)} %reduce.4), channel_id=1, replica_groups=mesh['seq'=8,'tp'=4] {'tp'}, use_global_device_ids=true, to_apply=%region_5.6 | all-reduce | flops 1024 | bytes 8192 | tf_op jit(solution)/shard_map/psum | solution.py:388
  323.5 30.9 %output_kernel.1 = f32[1024,512]{1,0:T(8,128)S(1)} custom-call(bf16[1024,1024]{1,0:T(8,128)(2,1)} %get-tuple-element.11.a_ref, bf16[1024,2048]{1,0:T(8,128)(2,1)} %all-gather.8.cloned.1.call-done.w_ref), custom_call_target="tpu_custom_call" | custom-call | tf_op jit(solution)/shard_map/output_kernel/pallas_call | solution.py:222
  354.3 1.3 select_convert_fusion
  (84 shorter events, 9.2 us)
Async XLA Ops:
  6.5 5.9 %copy-start.7 = (s32[32]{0:T(128)S(1)}, s32[32]{0:T(128)}, u32[]{:S(2)}) copy-start(s32[32]{0:T(128)} %param.24) | copy-start | bytes 388
  6.5 6.3 %copy-start.2 = (f32[4,1024]{1,0:T(4,128)S(1)}, f32[4,1024]{1,0:T(4,128)}, u32[]{:S(2)}) copy-start(f32[4,1024]{1,0:T(4,128)} %param.17) | copy-start | bytes 49156
  6.5 6.4 %copy-start.3 = (f32[4,256]{1,0:T(4,128)S(1)}, f32[4,256]{1,0:T(4,128)}, u32[]{:S(2)}) copy-start(f32[4,256]{1,0:T(4,128)} %param.18) | copy-start | bytes 12292
  6.5 6.4 %copy-start.6 = (f32[16]{0:T(128)S(1)}, f32[16]{0:T(128)}, u32[]{:S(2)}) copy-start(f32[16]{0:T(128)} %param.19) | copy-start | bytes 196
  6.5 6.4 %copy-start.8 = (s32[5]{0:T(128)S(1)}, s32[5]{0:T(128)}, u32[]{:S(2)}) copy-start(s32[5]{0:T(128)} %param.25) | copy-start | bytes 64
  6.5 37.9 %all-gather.6.cloned.1.call-start = ((), (), s32[]{:S(2)}) async-start(), calls=%async_computation.1 | async-start | bytes 5242880 | tf_op jit(solution)/shard_map/all_gather | solution.py:281
  7.3 180.9 %all-gather.4.cloned.1.call-start = ((), (), s32[]{:S(2)}) async-start(), calls=%async_computation | async-start | bytes 11206656 | tf_op jit(solution)/shard_map/all_gather | solution.py:285
  11.7 311.8 %all-gather.8.cloned.1.call-start = ((), (), s32[]{:S(2)}) async-start(), calls=%async_computation.2 | async-start | bytes 4718592 | tf_op jit(solution)/shard_map/all_gather | solution.py:390
  13.1 192.5 %copy-start.4 = (f32[16]{0:T(128)S(1)}, f32[16]{0:T(128)}, u32[]{:S(2)}) copy-start(f32[16]{0:T(128)} %param.20) | copy-start | bytes 196
  203.4 2.2 copy-start.1
  203.6 11.6 %collective-permute-start = (bf16[3,1280]{0,1:T(8,128)(2,1)S(1)}, bf16[3,1280]{0,1:T(8,128)(2,1)S(1)}, u32[]{:S(2)}, u32[]{:S(2)}) collective-permute-start(bf16[3,1280]{0,1:T(8,128)(2,1)S(1)} %slice.144), channel_id=1, source_target_pairs={{0,4},{4,8},{8,12},{12,16},{16,20},{20,24},{24,28},{1,5},{5,9},{9,... | collective-permute-start | bytes 23048 | tf_op jit(solution)/shard_map/ppermute | solution.py:16
  223.4 4.0 %slice-start = ((bf16[1024,2320]{0,1:T(8,128)(2,1)}), bf16[1024,256]{0,1:T(8,128)(2,1)S(1)}, s32[]{:S(2)}) async-start(bf16[1024,2320]{0,1:T(8,128)(2,1)} %copy-done.1), calls=%async_computation.3 | async-start | bytes 1048576 | tf_op jit(solution)/shard_map/slice | solution.py:289
  228.8 11.5 %copy-start.5 = (f32[16]{0:T(128)S(1)}, f32[16]{0:T(128)}, u32[]{:S(2)}) copy-start(f32[16]{0:T(128)} %param.21) | copy-start | bytes 196
  235.0 28.5 %collective-permute-start.3 = (bf16[144,1024]{1,0:T(8,128)(2,1)S(1)}, bf16[144,1024]{1,0:T(8,128)(2,1)S(1)}, u32[]{:S(2)}, u32[]{:S(2)}) collective-permute-start(bf16[144,1024]{1,0:T(8,128)(2,1)S(1)} %pad_maximum_fusion.1), channel_id=1, source_target_pairs={{0,12},{4,16},{8,20},{12,24},{16,28},{1,13},{5,17},{9,21},{13,25},... | collective-permute-start | bytes 884744 | tf_op jit(solution)/shard_map/ppermute | solution.py:16
  236.3 27.5 %collective-permute-start.2 = (bf16[144,1024]{1,0:T(8,128)(2,1)S(1)}, bf16[144,1024]{1,0:T(8,128)(2,1)S(1)}, u32[]{:S(2)}, u32[]{:S(2)}) collective-permute-start(bf16[144,1024]{1,0:T(8,128)(2,1)S(1)} %pad_maximum_fusion.1), channel_id=1, source_target_pairs={{0,8},{4,12},{8,16},{12,20},{16,24},{20,28},{1,9},{5,13},{9,17},{1... | collective-permute-start | bytes 884744 | tf_op jit(solution)/shard_map/ppermute | solution.py:16
  237.6 31.9 %collective-permute-start.1 = (bf16[144,1024]{1,0:T(8,128)(2,1)S(1)}, bf16[144,1024]{1,0:T(8,128)(2,1)S(1)}, u32[]{:S(2)}, u32[]{:S(2)}) collective-permute-start(bf16[144,1024]{1,0:T(8,128)(2,1)S(1)} %pad_maximum_fusion.1), channel_id=1, source_target_pairs={{0,4},{4,8},{8,12},{12,16},{16,20},{20,24},{24,28},{1,5},{5,9},{9,... | collective-permute-start | bytes 884744 | tf_op jit(solution)/shard_map/ppermute | solution.py:16
  239.0 67.0 %collective-permute-start.4 = (bf16[144,1024]{1,0:T(8,128)(2,1)S(1)}, bf16[144,1024]{1,0:T(8,128)(2,1)S(1)}, u32[]{:S(2)}, u32[]{:S(2)}) collective-permute-start(bf16[144,1024]{1,0:T(8,128)(2,1)S(1)} %pad_maximum_fusion.1), channel_id=1, source_target_pairs={{0,16},{4,20},{8,24},{12,28},{1,17},{5,21},{9,25},{13,29},{2,18},{... | collective-permute-start | bytes 884744 | tf_op jit(solution)/shard_map/ppermute | solution.py:16
  247.8 58.4 %copy-start = (f32[1024]{0:T(1024)S(1)}, f32[1024]{0:T(1024)}, u32[]{:S(2)}) copy-start(f32[1024]{0:T(1024)} %param.22) | copy-start | bytes 12292
Sparse Core Ops, SparseCore 0:
  8.9 35.4 all-gather.5
  46.6 141.5 all-gather.3
  190.2 97.1 all-gather.7

commit v3 on v2

--- a/solution.py
+++ b/solution.py
@@ -241,6 +241,168 @@
     )(rows, weights)
 
 
+def gather_kernel(
+    seq_count, tp_count, rows_ref, shard_ref, whole_ref, slots_ref, own_sem, line_sem, fan_sem,
+    slot_sem, peer_send, peer_recv
+):
+    mesh_id = pl.DeviceIdType.MESH
+    slow = 4 if seq_count % 4 == 0 else 1
+    fast = seq_count // slow
+    me = lax.axis_index("seq")
+    a, b = me // fast, lax.rem(me, fast)
+    t = lax.axis_index("tp")
+    width = rows_ref.shape[1]
+    barrier = pltpu.get_barrier_semaphore()
+
+    def greet(device):
+        pl.semaphore_signal(barrier, inc=1, device_id=device, device_id_type=mesh_id)
+
+    @pl.when(a > 0)
+    def _():
+        greet({"seq": me - fast})
+
+    @pl.when(a < slow - 1)
+    def _():
+        greet({"seq": me + fast})
+
+    for k in range(1, fast):
+        greet({"seq": a * fast + lax.rem(b + k, fast)})
+    for k in range(1, tp_count):
+        greet({"tp": lax.rem(t + k, tp_count)})
+
+    inside = (a > 0).astype(jnp.int32) + (a < slow - 1).astype(jnp.int32)
+    pl.semaphore_wait(barrier, inside + (fast - 1 + tp_count - 1))
+
+    def shard_copy(source, origin_a, origin_b, send_sem, target):
+        return pltpu.make_async_remote_copy(
+            src_ref=source,
+            dst_ref=slots_ref.at[origin_a * fast + origin_b],
+            send_sem=send_sem,
+            recv_sem=slot_sem.at[origin_a * fast + origin_b],
+            device_id={"seq": target},
+            device_id_type=mesh_id,
+        )
+
+    def to_right(source, origin):
+        return shard_copy(source, origin, b, line_sem.at[0, origin], me + fast)
+
+    def to_left(source, origin):
+        return shard_copy(source, origin, b, line_sem.at[1, origin], me - fast)
+
+    def to_fan(source, origin, k):
+        target = a * fast + lax.rem(b + k, fast)
+        return shard_copy(source, origin, b, fan_sem.at[origin, k - 1], target)
+
+    def peer_copy(k):
+        return pltpu.make_async_remote_copy(
+            src_ref=rows_ref,
+            dst_ref=whole_ref.at[:, pl.ds(pl.multiple_of(t * width, LANES), width)],
+            send_sem=peer_send.at[k - 1],
+            recv_sem=peer_recv.at[k - 1],
+            device_id={"tp": lax.rem(t + k, tp_count)},
+            device_id_type=mesh_id,
+        )
+
+    @pl.when(a < slow - 1)
+    def _():
+        to_right(shard_ref, a).start()
+
+    @pl.when(a > 0)
+    def _():
+        to_left(shard_ref, a).start()
+
+    for k in range(1, fast):
+        to_fan(shard_ref, a, k).start()
+    for k in range(1, tp_count):
+        peer_copy(k).start()
+    own_shard = pltpu.make_async_copy(shard_ref, slots_ref.at[me], own_sem.at[0])
+    own_rows = pltpu.make_async_copy(
+        rows_ref,
+        whole_ref.at[:, pl.ds(pl.multiple_of(t * width, LANES), width)],
+        own_sem.at[1],
+    )
+    own_shard.start()
+    own_rows.start()
+
+    for step in range(1, slow):
+
+        @pl.when(a - step >= 0)
+        def _():
+            origin = a - step
+            source = slots_ref.at[origin * fast + b]
+            to_right(source, origin).wait_recv()
+
+            @pl.when(a < slow - 1)
+            def _():
+                to_right(source, origin).start()
+
+            for k in range(1, fast):
+                to_fan(source, origin, k).start()
+
+        @pl.when(a + step < slow)
+        def _():
+            origin = a + step
+            source = slots_ref.at[origin * fast + b]
+            to_left(source, origin).wait_recv()
+
+            @pl.when(a > 0)
+            def _():
+                to_left(source, origin).start()
+
+            for k in range(1, fast):
+                to_fan(source, origin, k).start()
+
+    for origin in range(slow):
+        for k in range(1, fast):
+            sender = lax.rem(b + k, fast)
+            shard_copy(
+                shard_ref, origin, sender, fan_sem.at[origin, k - 1], a * fast + sender
+            ).wait_recv()
+            to_fan(shard_ref, origin, k).wait_send()
+
+        @pl.when((origin <= a) & (a < slow - 1))
+        def _():
+            to_right(shard_ref, origin).wait_send()
+
+        @pl.when((origin >= a) & (a > 0))
+        def _():
+            to_left(shard_ref, origin).wait_send()
+
+    for k in range(1, tp_count):
+        peer_copy(k).wait()
+    own_shard.wait()
+    own_rows.wait()
+
+
+def gathered(rows, shard, seq_count, tp_count):
+    slow = 4 if seq_count % 4 == 0 else 1
+    fast = seq_count // slow
+    anywhere = pl.BlockSpec(memory_space=pl.ANY)
+    dma = pltpu.SemaphoreType.DMA
+    whole, slots = pl.pallas_call(
+        functools.partial(gather_kernel, seq_count, tp_count),
+        out_shape=[
+            jax.ShapeDtypeStruct((rows.shape[0], rows.shape[1] * tp_count), rows.dtype),
+            jax.ShapeDtypeStruct((seq_count,) + shard.shape, shard.dtype),
+        ],
+        in_specs=[anywhere, anywhere],
+        out_specs=[anywhere, anywhere],
+        scratch_shapes=[
+            dma((2,)),
+            dma((2, slow)),
+            dma((slow, fast - 1)),
+            dma((seq_count,)),
+            dma((tp_count - 1,)),
+            dma((tp_count - 1,)),
+        ],
+        compiler_params=pltpu.CompilerParams(
+            collective_id=5, has_side_effects=True, vmem_limit_bytes=VMEM_BYTES
+        ),
+        name="gather_kernel",
+    )(rows, shard)
+    return whole, slots.reshape(seq_count * shard.shape[0], shard.shape[1])
+
+
 def on_device(
     tokens,
     w_inner,
@@ -278,16 +440,17 @@
     local_valid = lax.dynamic_slice_in_dim(valid_rows, seq_index * local_blocks, local_blocks)
     in_block = jnp.arange(row_count, dtype=jnp.int32) % BLOCK
     carry_on = jnp.repeat(local_start == 0, BLOCK)
-    whole = lax.all_gather(tokens, "tp", axis=1, tiled=True)
+    used = 2 * inner_here + 2 * state_size + heads_here
+    filler = jnp.zeros((w_step.shape[0], -used % LANES), w_step.dtype)
     shard = jnp.concatenate(
-        [w_inner.reshape(w_inner.shape[0], 2 * inner_here), w_states, w_step], axis=1
-    )
-    weights = lax.all_gather(shard, "seq", axis=0, tiled=True)
+        [w_inner.reshape(w_inner.shape[0], 2 * inner_here), w_states, w_step, filler], axis=1
+    )
+    whole, weights = gathered(tokens, shard, lax.axis_size("seq"), lax.axis_size("tp"))
     projected = jnp.dot(whole, weights, preferred_element_type=jnp.float32).astype(jnp.bfloat16)
     states_end = 2 * inner_here + 2 * state_size
     x_in = projected[:, inner_here : 2 * inner_here]
     bc_in = projected[:, 2 * inner_here : states_end]
-    step_raw = projected[:, states_end:]
+    step_raw = projected[:, states_end : states_end + heads_here]
     edges = passed_along(projected[row_count - lag_rows :, inner_here:states_end], "seq", 1)
     edge_inner, edge_states = edges[:, :inner_here], edges[:, inner_here:]
     x_conv = convolve(x_in, edge_inner, conv_inner, in_block, carry_on)

time: 363 us -> 321 us (0.88)
  waiting for transfers between devices: 237 us -> 30.6 us
  Pallas kernels: 46.8 us -> 210 us
  local copies, waits for them, and re-layouts: 19.3 us -> 23.4 us
    all_gather x2 -> x0, waiting for transfers between devices: 175 us -> none  [the longest x1 144 us: on_device(): weights = lax.all_gather(shard, 'seq', axis=0, tiled=True)]
    pallas_call x0 -> x1, Pallas kernels: none -> 163 us  [gathered(): pl.pallas_call(functools.partial(gather_kernel, seq_count, tp_count), out...]
    ppermute x5, waiting for transfers between devices: 60.7 us -> 29.8 us  [passed_along(): return lax.ppermute(value, axis, pairs)]
  transfers between devices with their start and end apart: 8 -> 6, of which waited for: 7 -> 2; matrix products, arithmetic and copies ran while one was open for 14% -> 16% of each run, Pallas kernels for 4% -> 56%
where the time goes in v3:
time: 321 us; the launch traced here: 320 us
  Pallas kernels  210 us (65%)
  waiting for transfers between devices  30.6 us (10%)
  local copies, waits for them, and re-layouts  23.4 us (7%)
  other arithmetic  15.3 us (5%)
  matrix products  15.1 us (5%)
  between operations  13.8 us (4%)
  starting transfers between devices  6.63 us (2%)
  blocking collectives  5.77 us (2%)
    pallas_call x1, Pallas kernels, gathered(): pl.pallas_call(functools.partial(gather_kernel, seq_count, tp_count), out...  163 us
    pallas_call x1, Pallas kernels, projected_sum(): pl.pallas_call(functools.partial(output_kernel, tp_count), out_shape=jax....  30.9 us
    ppermute x5, waiting for transfers between devices, passed_along(): return lax.ppermute(value, axis, pairs)  29.8 us
    dot_general x1, matrix products, on_device(): jnp.dot(whole, weights, preferred_element_type=jnp.float32)  15.1 us
    pallas_call x1, Pallas kernels, on_device(): pl.pallas_call(functools.partial(mix_kernel, head_size), grid=(local_bloc...  10.1 us
    convert_element_type x1, local copies, waits for them, and re-layouts, on_device(): jnp.dot(whole, weights, preferred_element_type=jnp.float32)  7.69 us
    convert_element_type x2, other arithmetic, convolve(): return jax.nn.silu(total).astype(jnp.bfloat16)  6.67 us
    ppermute x5, starting transfers between devices, passed_along(): return lax.ppermute(value, axis, pairs)  6.63 us
  transfers between devices with their start and end apart: 6, of which 2 were waited for; matrix products, arithmetic and copies ran while one was open for 16% of the time, Pallas kernels for 56%

profile of v3, /device:TPU:26, one launch (start us, length us, event | category | flops | bytes accessed | tf_op | source)
XLA Modules:
  0.0 320.1 jit_solution(11193424747130848655)
XLA Ops:
  7.3 1.5 copy.81
  9.6 2.0 concatenate.12.shard_ref
  11.6 162.7 %gather_kernel.1 = (bf16[1024,2048]{1,0:T(8,128)(2,1)}, bf16[8,256,2432]{2,1,0:T(8,128)(2,1)}) custom-call(bf16[1024,512]{1,0:T(8,128)(2,1)S(1)} %copy-done, bf16[256,2432]{1,0:T(8,128)(2,1)S(1)} %concatenate.12.shard_ref), custom_call_target="tpu_custom_call" | custom-call | tf_op jit(solution)/shard_map/gather_kernel/pallas_call | solution.py:382
  174.4 15.1 %convolution_convert_fusion = bf16[1024,2432]{0,1:T(8,128)(2,1)S(1)} fusion(bf16[1024,2048]{1,0:T(8,128)(2,1)} %get-tuple-element.11, bf16[2048,2432]{1,0:T(8,128)(2,1)} %bitcast.66), kind=kOutput, calls=%fused_computation | convolution fusion | flops 10203037696 | bytes 19136512 | tf_op jit(solution)/shard_map/dot_general | solution.py:449
  189.5 2.2 copy-done.2
  191.9 1.5 collective-permute-start
  194.6 2.3 reduce-window.6
  197.9 3.1 slice.146
  201.7 2.7 maximum_convert_fusion
  204.4 5.5 %multiply_convert_fusion = bf16[1024,1024]{0,1:T(8,128)(2,1)} fusion(f32[1027,1024]{0,1:T(8,128)S(1)} %maximum_convert_fusion, f32[1024]{0:T(1024)S(1)} %bitcast.59, f32[1024]{0:T(1024)S(1)} %bitcast.60, f32[1024]{0:T(1024)S(1)} %bitcast.58, f32[1024]{0:T(1024)S(1)} %bitcast.57, pred[1024]{0:T(1024)(128)(4,1)S(1)} %get-tuple-element.38, ...), kind=kLoop, calls=%fused_computation.12 | loop fusion | flops 16777216 | bytes 18894848 | tf_op jit(solution)/shard_map/convert_element_type | solution.py:28
  209.9 4.0 %copy.71.x_ref = bf16[1024,1024]{1,0:T(8,128)(2,1)} copy(bf16[1024,1024]{0,1:T(8,128)(2,1)} %multiply_convert_fusion) | data formatting | bytes 4194304 | tf_op jit(solution)/shard_map/convert_element_type | solution.py:28
  214.2 1.2 multiply_convert_fusion.1
  215.6 5.9 %state_kernel.1 = (f32[4,128,1024]{2,1,0:T(8,128)}, f32[128,1024]{1,0:T(8,128)S(1)}) custom-call(bf16[1024,1024]{1,0:T(8,128)(2,1)} %copy.71.x_ref, bf16[1024,256]{1,0:T(8,128)(2,1)S(1)} %copy.72.bc_ref, f32[1024,16]{1,0:T(8,128)S(1)} %copy.74.cum_ref, f32[1024,16]{1,0:T(8,128)S(1)} %copy.70.step_ref, f32[4,1,1024]{2,1,0:T(1,128)S(1)} %broadcast_in_dim_reshape.6.gain_ref), custom_call_target="tpu_custom_call" | custom-call | tf_op jit(solution)/shard_map/state_kernel/pallas_call | solution.py:472
  221.5 1.3 collective-permute-start.3
  222.8 1.3 collective-permute-start.2
  224.1 1.3 collective-permute-start.1
  225.5 1.3 collective-permute-start.4
  226.8 7.7 %copy.73.gate_ref = bf16[1024,2432]{1,0:T(8,128)(2,1)} copy(bf16[1024,2432]{0,1:T(8,128)(2,1)} %copy-done.2) | data formatting | bytes 9961472 | tf_op jit(solution)/shard_map/convert_element_type | solution.py:449
  234.7 6.3 %collective-permute-done.2 = bf16[144,1024]{1,0:T(8,128)(2,1)S(1)} collective-permute-done((bf16[144,1024]{1,0:T(8,128)(2,1)S(1)}, bf16[144,1024]{1,0:T(8,128)(2,1)S(1)}, u32[]{:S(2)}, u32[]{:S(2)}) %collective-permute-start.2) | collective-permute-done | bytes 294944 | tf_op jit(solution)/shard_map/ppermute | solution.py:16
  241.1 23.6 %collective-permute-done.4 = bf16[144,1024]{1,0:T(8,128)(2,1)S(1)} collective-permute-done((bf16[144,1024]{1,0:T(8,128)(2,1)S(1)}, bf16[144,1024]{1,0:T(8,128)(2,1)S(1)}, u32[]{:S(2)}, u32[]{:S(2)}) %collective-permute-start.4) | collective-permute-done | bytes 294944 | tf_op jit(solution)/shard_map/ppermute | solution.py:16
  265.0 10.1 %mix_kernel.1 = (bf16[1024,1024]{1,0:T(8,128)(2,1)}, f32[1024,1]{1,0:T(8,128)S(1)}) custom-call(bf16[1024,1024]{1,0:T(8,128)(2,1)} %copy.71.x_ref, bf16[1024,256]{1,0:T(8,128)(2,1)S(1)} %copy.72.bc_ref, bf16[1024,2432]{1,0:T(8,128)(2,1)} %copy.73.gate_ref, f32[1024,16]{1,0:T(8,128)S(1)} %copy.74.cum_ref, f32[16,1024]{1,0:T(8,128)S(1)} %bitcast.49, ...), custom_call_target="tpu_custom_call" | custom-call | tf_op jit(solution)/shard_map/mix_kernel/pallas_call | solution.py:511
  275.3 5.8 %psum.7 = f32[1024]{0:T(1024)S(1)} all-reduce(f32[1024]{0:T(1024)S(1)} %reduce.4), channel_id=1, replica_groups=mesh['seq'=8,'tp'=4] {'tp'}, use_global_device_ids=true, to_apply=%region_5.6 | all-reduce | flops 1024 | bytes 8192 | tf_op jit(solution)/shard_map/psum | solution.py:551
  281.1 30.9 %output_kernel.1 = f32[1024,512]{1,0:T(8,128)S(1)} custom-call(bf16[1024,1024]{1,0:T(8,128)(2,1)} %get-tuple-element.15.a_ref, bf16[1024,2048]{1,0:T(8,128)(2,1)} %all-gather.2.cloned.1.call-done.w_ref), custom_call_target="tpu_custom_call" | custom-call | tf_op jit(solution)/shard_map/output_kernel/pallas_call | solution.py:222
  311.9 1.3 select_convert_fusion
  (82 shorter events, 6.0 us)
Async XLA Ops:
  6.5 5.1 %copy-start = (bf16[1024,512]{1,0:T(8,128)(2,1)S(1)}, bf16[1024,512]{1,0:T(8,128)(2,1)}, u32[]{:S(2)}) copy-start(bf16[1024,512]{1,0:T(8,128)(2,1)} %rows_ref.1) | copy-start | bytes 3145732
  6.5 274.5 %all-gather.2.cloned.1.call-start = ((), (), s32[]{:S(2)}) async-start(), calls=%async_computation | async-start | bytes 4718592 | tf_op jit(solution)/shard_map/all_gather | solution.py:553
  174.3 19.1 %copy-start.8 = (s32[32]{0:T(128)S(1)}, s32[32]{0:T(128)}, u32[]{:S(2)}) copy-start(s32[32]{0:T(128)} %param.24) | copy-start | bytes 388
  174.3 19.4 %copy-start.7 = (f32[16]{0:T(128)S(1)}, f32[16]{0:T(128)}, u32[]{:S(2)}) copy-start(f32[16]{0:T(128)} %param.19) | copy-start | bytes 196
  174.3 19.4 %copy-start.5 = (f32[16]{0:T(128)S(1)}, f32[16]{0:T(128)}, u32[]{:S(2)}) copy-start(f32[16]{0:T(128)} %param.20) | copy-start | bytes 196
  174.4 23.4 %copy-start.9 = (s32[5]{0:T(128)S(1)}, s32[5]{0:T(128)}, u32[]{:S(2)}) copy-start(s32[5]{0:T(128)} %param.25) | copy-start | bytes 64
  174.4 23.5 %copy-start.4 = (f32[4,256]{1,0:T(4,128)S(1)}, f32[4,256]{1,0:T(4,128)}, u32[]{:S(2)}) copy-start(f32[4,256]{1,0:T(4,128)} %param.18) | copy-start | bytes 12292
  174.4 23.5 %copy-start.3 = (f32[4,1024]{1,0:T(4,128)S(1)}, f32[4,1024]{1,0:T(4,128)}, u32[]{:S(2)}) copy-start(f32[4,1024]{1,0:T(4,128)} %param.17) | copy-start | bytes 49156
  189.5 2.2 copy-start.2
  191.9 9.8 %collective-permute-start = (bf16[3,1280]{0,1:T(8,128)(2,1)S(1)}, bf16[3,1280]{0,1:T(8,128)(2,1)S(1)}, u32[]{:S(2)}, u32[]{:S(2)}) collective-permute-start(bf16[3,1280]{0,1:T(8,128)(2,1)S(1)} %slice.144), channel_id=1, source_target_pairs={{0,4},{4,8},{8,12},{12,16},{16,20},{20,24},{24,28},{1,5},{5,9},{9,... | collective-permute-start | bytes 23048 | tf_op jit(solution)/shard_map/ppermute | solution.py:16
  209.9 4.0 %slice-start = ((bf16[1024,2432]{0,1:T(8,128)(2,1)}), bf16[1024,256]{0,1:T(8,128)(2,1)S(1)}, s32[]{:S(2)}) async-start(bf16[1024,2432]{0,1:T(8,128)(2,1)} %copy-done.2), calls=%async_computation.1 | async-start | bytes 1048576 | tf_op jit(solution)/shard_map/slice | solution.py:452
  221.5 13.1 %collective-permute-start.3 = (bf16[144,1024]{1,0:T(8,128)(2,1)S(1)}, bf16[144,1024]{1,0:T(8,128)(2,1)S(1)}, u32[]{:S(2)}, u32[]{:S(2)}) collective-permute-start(bf16[144,1024]{1,0:T(8,128)(2,1)S(1)} %pad_maximum_fusion), channel_id=1, source_target_pairs={{0,12},{4,16},{8,20},{12,24},{16,28},{1,13},{5,17},{9,21},{13,25},... | collective-permute-start | bytes 884744 | tf_op jit(solution)/shard_map/ppermute | solution.py:16
  222.8 18.2 %collective-permute-start.2 = (bf16[144,1024]{1,0:T(8,128)(2,1)S(1)}, bf16[144,1024]{1,0:T(8,128)(2,1)S(1)}, u32[]{:S(2)}, u32[]{:S(2)}) collective-permute-start(bf16[144,1024]{1,0:T(8,128)(2,1)S(1)} %pad_maximum_fusion), channel_id=1, source_target_pairs={{0,8},{4,12},{8,16},{12,20},{16,24},{20,28},{1,9},{5,13},{9,17},{1... | collective-permute-start | bytes 884744 | tf_op jit(solution)/shard_map/ppermute | solution.py:16
  224.1 16.9 %collective-permute-start.1 = (bf16[144,1024]{1,0:T(8,128)(2,1)S(1)}, bf16[144,1024]{1,0:T(8,128)(2,1)S(1)}, u32[]{:S(2)}, u32[]{:S(2)}) collective-permute-start(bf16[144,1024]{1,0:T(8,128)(2,1)S(1)} %pad_maximum_fusion), channel_id=1, source_target_pairs={{0,4},{4,8},{8,12},{12,16},{16,20},{20,24},{24,28},{1,5},{5,9},{9,... | collective-permute-start | bytes 884744 | tf_op jit(solution)/shard_map/ppermute | solution.py:16
  225.5 39.2 %collective-permute-start.4 = (bf16[144,1024]{1,0:T(8,128)(2,1)S(1)}, bf16[144,1024]{1,0:T(8,128)(2,1)S(1)}, u32[]{:S(2)}, u32[]{:S(2)}) collective-permute-start(bf16[144,1024]{1,0:T(8,128)(2,1)S(1)} %pad_maximum_fusion), channel_id=1, source_target_pairs={{0,16},{4,20},{8,24},{12,28},{1,17},{5,21},{9,25},{13,29},{2,18},{... | collective-permute-start | bytes 884744 | tf_op jit(solution)/shard_map/ppermute | solution.py:16
  226.8 7.7 %copy-start.6 = (f32[16]{0:T(128)S(1)}, f32[16]{0:T(128)}, u32[]{:S(2)}) copy-start(f32[16]{0:T(128)} %param.21) | copy-start | bytes 196
  234.5 30.4 %copy-start.1 = (f32[1024]{0:T(1024)S(1)}, f32[1024]{0:T(1024)}, u32[]{:S(2)}) copy-start(f32[1024]{0:T(1024)} %param.22) | copy-start | bytes 12292
Sparse Core Ops, SparseCore 0:
  9.4 118.4 all-gather.1
